TPU v7x, 1024 devices: a whole 4x8x16 slice. The times are simulated.
1024 devices in a mesh: group: 8 (over y), local: 128 (over z, x, core).
Axes of the slice: x: 4, y: 8, z: 16, core: 2. Of those that a mesh axis runs over, the one named last changes fastest.
Arguments:
- grad_out: bfloat16 [4096, 7168], P('group', 'local'), may hold values from -6 to 6
- tokens_in: bfloat16 [4096, 7168], P('group', 'local'), may hold values from -6 to 6
- expert_ids: int32 [4096, 8], P('group'), may hold values from 0 to 255, as said below
- gate_values: float32 [4096, 8], P('group'), may hold values from 0.05 to 0.6
- w_gate: bfloat16 [8, 128, 448, 256], P('group', 'local'), may hold values from -0.0625 to 0.0625
- w_up: bfloat16 [8, 128, 448, 256], P('group', 'local'), may hold values from -0.0625 to 0.0625
- w_down_t: bfloat16 [8, 128, 448, 256], P('group', 'local'), may hold values from -0.125 to 0.125
Outputs:
- grad_tokens: bfloat16 [4096, 7168], P('group', 'local')
- grad_gate: float32 [8, 128, 448, 256], P('group', 'local')
- grad_up: float32 [8, 128, 448, 256], P('group', 'local')
- grad_down_t: float32 [8, 128, 448, 256], P('group', 'local')
Inputs may be any that keep to these rules, and one draw needn't show every extreme that they name: `expert_ids`: each token names 8 different experts, all from at most 4 groups (expert e belongs to group e // 32), and at most one first expert of a group. Of the 512 tokens of one group at most 32 name the first expert of any one group; this number is reached for some group from the tokens of every group, and for one group from the tokens of all groups.
All inputs are finite; a program needn't handle non-finite values.
Results may differ from a plain program's by a relative error of at most 0.0057.
Values may be sent and summed in bfloat16 or wider, within the bound.
A program may use at most 32 MiB of HBM per device.

v0:
```python
import jax
import jax.numpy as jnp
from jax import lax
from jax.sharding import PartitionSpec as P

EXP_GRP = 32
CAP = 32


def from_partner(value, axis, apart):
    return lax.ppermute(value, axis, [(i, i ^ 1 << apart) for i in range(lax.axis_size(axis))])


def gate_backward(pre_gate, pre_up, grad_hidden):
    sigma = jax.nn.sigmoid(pre_gate)
    hidden = (pre_gate * sigma * pre_up).astype(jnp.bfloat16)
    d_gate = (grad_hidden * pre_up * sigma * (1.0 + pre_gate * (1.0 - sigma))).astype(jnp.bfloat16)
    d_up = (grad_hidden * pre_gate * sigma).astype(jnp.bfloat16)
    return jnp.stack([d_gate, d_up, hidden])


def contract_last(left, right):
    return lax.dot_general(
        left, right, (((1,), (1,)), ((), ())), preferred_element_type=jnp.float32
    )


def contract_first(left, right):
    return lax.dot_general(
        left, right, (((0,), (0,)), ((), ())), preferred_element_type=jnp.float32
    )


def join_sides(mine, other, low_side, axis_num):
    lower = jnp.where(low_side, mine, other)
    upper = jnp.where(low_side, other, mine)
    return jnp.concatenate([lower, upper], axis=axis_num)


def per_device(grad_out, tokens_in, expert_ids, gate_values, w_gate, w_up, w_down_t):
    group_count = lax.axis_size("group")
    local_count = lax.axis_size("local")
    local_index = lax.axis_index("local")
    token_count, col_count = grad_out.shape
    feat_rows = w_gate.shape[2]
    split_count = local_count * col_count // feat_rows
    block_count = local_count // split_count
    hid_bits = block_count.bit_length() - 1
    feat_bits = split_count.bit_length() - 1
    targets = jnp.arange(group_count, dtype=jnp.int32) * EXP_GRP
    matches = expert_ids[:, :, None] == targets[None, None, :]
    hit_mask = jnp.any(matches, axis=1)
    gate_table = jnp.sum(jnp.where(matches, gate_values[:, :, None], jnp.float32(0.0)), axis=1)
    token_rank = jnp.cumsum(hit_mask.astype(jnp.int32), axis=0) - 1
    slot_index = jnp.where(hit_mask, token_rank, CAP)
    token_index = jnp.broadcast_to(
        jnp.arange(token_count, dtype=jnp.int32)[:, None], hit_mask.shape
    )
    group_index = jnp.broadcast_to(
        jnp.arange(group_count, dtype=jnp.int32)[None, :], hit_mask.shape
    )
    slot_table = jnp.full((group_count, CAP), token_count, jnp.int32)
    slot_table = slot_table.at[group_index, slot_index].set(token_index, mode="drop")
    padded_gate = jnp.concatenate([gate_table, jnp.zeros((1, group_count), jnp.float32)], axis=0)
    slot_gate = padded_gate[slot_table, jnp.arange(group_count, dtype=jnp.int32)[:, None]]
    dy_rows = jnp.take(grad_out, slot_table, axis=0, mode="fill", fill_value=0)
    x_rows = jnp.take(tokens_in, slot_table, axis=0, mode="fill", fill_value=0)
    scaled = (slot_gate[:, :, None] * dy_rows.astype(jnp.float32)).astype(jnp.bfloat16)
    recv_x, recv_scaled = (
        lax.all_to_all(x_rows, "group", split_axis=0, concat_axis=0, tiled=True),
        lax.all_to_all(scaled, "group", split_axis=0, concat_axis=0, tiled=True),
    )
    slot_count = group_count * CAP
    widened = jnp.stack(
        [recv_x.reshape(slot_count, col_count), recv_scaled.reshape(slot_count, col_count)]
    )
    for bit_num in range(hid_bits):
        partner = from_partner(widened, "local", bit_num)
        low_side = local_index >> bit_num & 1 == 0
        widened = join_sides(widened, partner, low_side, 2)
    x_block = widened[0]
    scaled_block = widened[1]
    gate_block = w_gate[0, 0]
    up_block = w_up[0, 0]
    down_block = w_down_t[0, 0]
    partials = jnp.stack(
        [
            jnp.dot(x_block, gate_block, preferred_element_type=jnp.float32),
            jnp.dot(x_block, up_block, preferred_element_type=jnp.float32),
            jnp.dot(scaled_block, down_block, preferred_element_type=jnp.float32),
        ]
    )
    for bit_num in range(hid_bits, hid_bits + feat_bits):
        partials = partials + from_partner(partials, "local", bit_num)
    results = gate_backward(partials[0], partials[1], partials[2])
    d_gate = results[0]
    d_up = results[1]
    hidden = results[2]
    returned = contract_last(d_gate, gate_block) + contract_last(d_up, up_block)
    grad_gate = contract_first(x_block, d_gate)
    grad_up = contract_first(x_block, d_up)
    grad_down = contract_first(scaled_block, hidden)
    for bit_num in reversed(range(hid_bits)):
        half_size = returned.shape[1] // 2
        low_side = local_index >> bit_num & 1 == 0
        kept_half = jnp.where(low_side, returned[:, :half_size], returned[:, half_size:])
        sent_half = jnp.where(low_side, returned[:, half_size:], returned[:, :half_size])
        returned = kept_half + from_partner(sent_half, "local", bit_num)
    home_rows = lax.all_to_all(
        returned.reshape(group_count, CAP, col_count).astype(jnp.bfloat16),
        "group",
        split_axis=0,
        concat_axis=0,
        tiled=True,
    ).astype(jnp.float32)
    grad_tokens = (
        jnp.zeros((token_count, col_count), jnp.float32).at[slot_table].add(home_rows, mode="drop")
    )
    return (
        grad_tokens.astype(jnp.bfloat16),
        grad_gate[None, None],
        grad_up[None, None],
        grad_down[None, None],
    )


def solution(mesh):
    placed = (
        P("group", "local"),
        P("group", "local"),
        P("group", None),
        P("group", None),
        P("group", "local", None, None),
        P("group", "local", None, None),
        P("group", "local", None, None),
    )
    return jax.shard_map(
        per_device,
        mesh=mesh,
        in_specs=placed,
        out_specs=(
            P("group", "local"),
            P("group", "local", None, None),
            P("group", "local", None, None),
            P("group", "local", None, None),
        ),
        check_vma=False,
    )
```

profile of v0, /device:TPU:194, one launch (start us, length us, event | category | flops | bytes accessed | tf_op | source)
XLA Modules:
  0.0 318.7 jit_solution(1719929500115947550)
XLA Ops:
  4.9 15.5 %scatter_custom_fusion.1 = s32[256]{0:T(256)S(1)} fusion(s32[4096]{0:T(1024)S(1)} %reshape.89, s32[4096]{0:T(1024)S(1)} %reshape.91, s32[]{:T(128)} %constant.20.clone.1), kind=kCustom, calls=%fused_computation.74 | custom fusion | bytes 1028
  22.4 7.2 %all-to-all-start = ((bf16[8,2,896]{2,1,0:T(2,128)(2,1)}), bf16[8,2,896]{2,1,0:T(2,128)(2,1)S(1)}, u32[]{:S(2)}, u32[]{:S(2)}) async-start(bf16[8,2,896]{2,1,0:T(2,128)(2,1)} %reshape.121), calls=%async_computation | async-start | bytes 57344 | tf_op jit(solution)/shard_map/all_to_all | solution.py:70
  30.2 1.9 gather_fusion
  33.9 3.7 %all-to-all-done = bf16[8,2,896]{2,1,0:T(2,128)(2,1)S(1)} async-done(((bf16[8,2,896]{2,1,0:T(2,128)(2,1)}), bf16[8,2,896]{2,1,0:T(2,128)(2,1)S(1)}, u32[]{:S(2)}, u32[]{:S(2)}) %all-to-all-start) | async-done | bytes 28704 | tf_op jit(solution)/shard_map/all_to_all | solution.py:70
  37.6 3.5 %all-to-all-start.1 = ((bf16[8,2,896]{2,1,0:T(2,128)(2,1)}), bf16[8,2,896]{2,1,0:T(2,128)(2,1)S(1)}, u32[]{:S(2)}, u32[]{:S(2)}) async-start(bf16[8,2,896]{2,1,0:T(2,128)(2,1)} %reshape.119), calls=%async_computation.1 | async-start | bytes 57344 | tf_op jit(solution)/shard_map/all_to_all | solution.py:71
  41.4 7.7 %all-to-all-done.1 = bf16[8,2,896]{2,1,0:T(2,128)(2,1)S(1)} async-done(((bf16[8,2,896]{2,1,0:T(2,128)(2,1)}), bf16[8,2,896]{2,1,0:T(2,128)(2,1)S(1)}, u32[]{:S(2)}, u32[]{:S(2)}) %all-to-all-start.1) | async-done | bytes 28704 | tf_op jit(solution)/shard_map/all_to_all | solution.py:71
  49.4 1.9 collective-permute-start
  52.6 2.4 collective-permute-start.1
  55.0 4.6 %collective-permute-done.1 = bf16[2,256,112]{1,2,0:T(8,128)(2,1)S(1)} collective-permute-done((bf16[2,256,112]{1,2,0:T(8,128)(2,1)S(1)}, bf16[2,256,112]{1,2,0:T(8,128)(2,1)S(1)}, u32[]{:S(2)}, u32[]{:S(2)}) %collective-permute-start.1) | collective-permute-done | bytes 114720 | tf_op jit(solution)/shard_map/ppermute | solution.py:11
  59.7 4.0 %collective-permute-start.2 = (bf16[2,256,224]{1,2,0:T(8,128)(2,1)S(1)}, bf16[2,256,224]{1,2,0:T(8,128)(2,1)S(1)}, u32[]{:S(2)}, u32[]{:S(2)}) collective-permute-start(bf16[2,256,224]{1,2,0:T(8,128)(2,1)S(1)} %pad_maximum_fusion.2), channel_id=1, source_target_pairs={{0,4},{1,5},{2,6},{3,7},{4,0},{5,1},{6,2},{7,3},{8,12},{9,13},{10,... | collective-permute-start | bytes 688136 | tf_op jit(solution)/shard_map/ppermute | solution.py:11
  63.8 6.2 %collective-permute-done.2 = bf16[2,256,224]{1,2,0:T(8,128)(2,1)S(1)} collective-permute-done((bf16[2,256,224]{1,2,0:T(8,128)(2,1)S(1)}, bf16[2,256,224]{1,2,0:T(8,128)(2,1)S(1)}, u32[]{:S(2)}, u32[]{:S(2)}) %collective-permute-start.2) | collective-permute-done | bytes 229408 | tf_op jit(solution)/shard_map/ppermute | solution.py:11
  74.5 17.8 %collective-permute-done.3 = f32[3,256,256]{2,1,0:T(8,128)S(1)} collective-permute-done((f32[3,256,256]{2,1,0:T(8,128)S(1)}, f32[3,256,256]{2,1,0:T(8,128)S(1)}, u32[]{:S(2)}, u32[]{:S(2)}) %collective-permute-start.3) | collective-permute-done | bytes 786464 | tf_op jit(solution)/shard_map/ppermute | solution.py:11
  92.4 6.8 %collective-permute-start.4 = (f32[3,256,256]{2,1,0:T(8,128)S(1)}, f32[3,256,256]{2,1,0:T(8,128)S(1)}, u32[]{:S(2)}, u32[]{:S(2)}) collective-permute-start(f32[3,256,256]{2,1,0:T(8,128)S(1)} %fusion.30), channel_id=1, source_target_pairs={{0,16},{1,17},{2,18},{3,19},{4,20},{5,21},{6,22},{7,23},{8,24},{9,... | collective-permute-start | bytes 2359304 | tf_op jit(solution)/shard_map/ppermute | solution.py:11
  99.3 32.7 %collective-permute-done.4 = f32[3,256,256]{2,1,0:T(8,128)S(1)} collective-permute-done((f32[3,256,256]{2,1,0:T(8,128)S(1)}, f32[3,256,256]{2,1,0:T(8,128)S(1)}, u32[]{:S(2)}, u32[]{:S(2)}) %collective-permute-start.4) | collective-permute-done | bytes 786464 | tf_op jit(solution)/shard_map/ppermute | solution.py:11
  132.1 8.0 %collective-permute-start.5 = (f32[3,256,256]{2,1,0:T(8,128)S(1)}, f32[3,256,256]{2,1,0:T(8,128)S(1)}, u32[]{:S(2)}, u32[]{:S(2)}) collective-permute-start(f32[3,256,256]{2,1,0:T(8,128)S(1)} %fusion.35), channel_id=1, source_target_pairs={{0,32},{1,33},{2,34},{3,35},{4,36},{5,37},{6,38},{7,39},{8,40},{9,... | collective-permute-start | bytes 2359304 | tf_op jit(solution)/shard_map/ppermute | solution.py:11
  140.1 80.5 %collective-permute-done.5 = f32[3,256,256]{2,1,0:T(8,128)S(1)} collective-permute-done((f32[3,256,256]{2,1,0:T(8,128)S(1)}, f32[3,256,256]{2,1,0:T(8,128)S(1)}, u32[]{:S(2)}, u32[]{:S(2)}) %collective-permute-start.5) | collective-permute-done | bytes 786464 | tf_op jit(solution)/shard_map/ppermute | solution.py:11
  220.7 12.1 %collective-permute-start.6 = (f32[3,256,256]{2,1,0:T(8,128)S(1)}, f32[3,256,256]{2,1,0:T(8,128)S(1)}, u32[]{:S(2)}, u32[]{:S(2)}) collective-permute-start(f32[3,256,256]{2,1,0:T(8,128)S(1)} %add.73), channel_id=1, source_target_pairs={{0,64},{1,65},{2,66},{3,67},{4,68},{5,69},{6,70},{7,71},{8,72},{9,... | collective-permute-start | bytes 2359304 | tf_op jit(solution)/shard_map/ppermute | solution.py:11
  232.8 49.8 %collective-permute-done.6 = f32[3,256,256]{2,1,0:T(8,128)S(1)} collective-permute-done((f32[3,256,256]{2,1,0:T(8,128)S(1)}, f32[3,256,256]{2,1,0:T(8,128)S(1)}, u32[]{:S(2)}, u32[]{:S(2)}) %collective-permute-start.6) | collective-permute-done | bytes 786464 | tf_op jit(solution)/shard_map/ppermute | solution.py:11
  283.3 4.0 %collective-permute-start.7 = (f32[256,224]{0,1:T(8,128)S(1)}, f32[256,224]{0,1:T(8,128)S(1)}, u32[]{:S(2)}, u32[]{:S(2)}) collective-permute-start(f32[256,224]{0,1:T(8,128)S(1)} %slice_select_fusion), channel_id=1, source_target_pairs={{0,4},{1,5},{2,6},{3,7},{4,0},{5,1},{6,2},{7,3},{8,12},{9,13},{10,... | collective-permute-start | bytes 688136 | tf_op jit(solution)/shard_map/ppermute | solution.py:11
  287.4 6.9 %collective-permute-done.7 = f32[256,224]{0,1:T(8,128)S(1)} collective-permute-done((f32[256,224]{0,1:T(8,128)S(1)}, f32[256,224]{0,1:T(8,128)S(1)}, u32[]{:S(2)}, u32[]{:S(2)}) %collective-permute-start.7) | collective-permute-done | bytes 229408 | tf_op jit(solution)/shard_map/ppermute | solution.py:11
  294.3 2.4 collective-permute-start.8
  297.8 3.2 %collective-permute-done.8 = f32[256,112]{0,1:T(8,128)S(1)} collective-permute-done((f32[256,112]{0,1:T(8,128)S(1)}, f32[256,112]{0,1:T(8,128)S(1)}, u32[]{:S(2)}, u32[]{:S(2)}) %collective-permute-start.8) | collective-permute-done | bytes 114720 | tf_op jit(solution)/shard_map/ppermute | solution.py:11
  305.1 3.3 %all-to-all-start.2 = ((bf16[8,2,896]{2,1,0:T(2,128)(2,1)}), bf16[8,2,896]{2,1,0:T(2,128)(2,1)S(1)}, u32[]{:S(2)}, u32[]{:S(2)}) async-start(bf16[8,2,896]{2,1,0:T(2,128)(2,1)} %reshape.123), calls=%async_computation.2 | async-start | bytes 57344 | tf_op jit(solution)/shard_map/all_to_all | solution.py:109
  309.4 6.9 %all-to-all-done.2 = bf16[8,2,896]{2,1,0:T(2,128)(2,1)S(1)} async-done(((bf16[8,2,896]{2,1,0:T(2,128)(2,1)}), bf16[8,2,896]{2,1,0:T(2,128)(2,1)S(1)}, u32[]{:S(2)}, u32[]{:S(2)}) %all-to-all-start.2) | async-done | bytes 28704 | tf_op jit(solution)/shard_map/all_to_all | solution.py:109
  (94 shorter events, 24.3 us)
Async XLA Ops:
  0.6 70.7 %copy-start = (bf16[1,1,448,256]{3,2,1,0:T(8,128)(2,1)S(1)}, bf16[1,1,448,256]{3,2,1,0:T(8,128)(2,1)}, u32[]{:S(2)}) copy-start(bf16[1,1,448,256]{3,2,1,0:T(8,128)(2,1)} %param.13) | copy-start | bytes 688132
  3.0 0.7 copy-start.8
  3.7 0.7 copy-start.7
  4.7 15.8 %copy-start.4 = (bf16[512,56]{0,1:T(8,128)(2,1)S(1)}, bf16[512,56]{0,1:T(8,128)(2,1)}, u32[]{:S(2)}) copy-start(bf16[512,56]{0,1:T(8,128)(2,1)} %param.10) | copy-start | bytes 172036
  21.7 8.0 %copy-start.6 = (f32[512,8]{0,1:T(8,128)S(1)}, f32[512,8]{0,1:T(8,128)}, u32[]{:S(2)}) copy-start(f32[512,8]{0,1:T(8,128)} %param.12) | copy-start | bytes 49156
  22.4 7.3 %copy-start.3 = (s32[512,8]{0,1:T(8,128)S(1)}, s32[512,8]{0,1:T(8,128)}, u32[]{:S(2)}) copy-start(s32[512,8]{0,1:T(8,128)} %param.11) | copy-start | bytes 49156
  22.4 7.4 %copy-start.5 = (bf16[512,56]{0,1:T(8,128)(2,1)S(1)}, bf16[512,56]{0,1:T(8,128)(2,1)}, u32[]{:S(2)}) copy-start(bf16[512,56]{0,1:T(8,128)(2,1)} %param.9) | copy-start | bytes 172036
  22.4 15.2 %all-to-all-start = ((bf16[8,2,896]{2,1,0:T(2,128)(2,1)}), bf16[8,2,896]{2,1,0:T(2,128)(2,1)S(1)}, u32[]{:S(2)}, u32[]{:S(2)}) async-start(bf16[8,2,896]{2,1,0:T(2,128)(2,1)} %reshape.121), calls=%async_computation | async-start | bytes 57344 | tf_op jit(solution)/shard_map/all_to_all | solution.py:70
  37.6 11.5 %all-to-all-start.1 = ((bf16[8,2,896]{2,1,0:T(2,128)(2,1)}), bf16[8,2,896]{2,1,0:T(2,128)(2,1)S(1)}, u32[]{:S(2)}, u32[]{:S(2)}) async-start(bf16[8,2,896]{2,1,0:T(2,128)(2,1)} %reshape.119), calls=%async_computation.1 | async-start | bytes 57344 | tf_op jit(solution)/shard_map/all_to_all | solution.py:71
  49.4 3.1 collective-permute-start
  52.6 7.1 %collective-permute-start.1 = (bf16[2,256,112]{1,2,0:T(8,128)(2,1)S(1)}, bf16[2,256,112]{1,2,0:T(8,128)(2,1)S(1)}, u32[]{:S(2)}, u32[]{:S(2)}) collective-permute-start(bf16[2,256,112]{1,2,0:T(8,128)(2,1)S(1)} %pad_maximum_fusion.3), channel_id=1, source_target_pairs={{0,2},{1,3},{2,0},{3,1},{4,6},{5,7},{6,4},{7,5},{8,10},{9,11},{10,... | collective-permute-start | bytes 344072 | tf_op jit(solution)/shard_map/ppermute | solution.py:11
  59.7 10.2 %collective-permute-start.2 = (bf16[2,256,224]{1,2,0:T(8,128)(2,1)S(1)}, bf16[2,256,224]{1,2,0:T(8,128)(2,1)S(1)}, u32[]{:S(2)}, u32[]{:S(2)}) collective-permute-start(bf16[2,256,224]{1,2,0:T(8,128)(2,1)S(1)} %pad_maximum_fusion.2), channel_id=1, source_target_pairs={{0,4},{1,5},{2,6},{3,7},{4,0},{5,1},{6,2},{7,3},{8,12},{9,13},{10,... | collective-permute-start | bytes 688136 | tf_op jit(solution)/shard_map/ppermute | solution.py:11
  70.1 0.9 copy-start.1
  71.3 0.9 copy-start.2
  72.6 19.7 %collective-permute-start.3 = (f32[3,256,256]{2,1,0:T(8,128)S(1)}, f32[3,256,256]{2,1,0:T(8,128)S(1)}, u32[]{:S(2)}, u32[]{:S(2)}) collective-permute-start(f32[3,256,256]{2,1,0:T(8,128)S(1)} %pad_maximum_fusion), channel_id=1, source_target_pairs={{0,8},{1,9},{2,10},{3,11},{4,12},{5,13},{6,14},{7,15},{8,0},{9,1},... | collective-permute-start | bytes 2359304 | tf_op jit(solution)/shard_map/ppermute | solution.py:11
  92.4 39.5 %collective-permute-start.4 = (f32[3,256,256]{2,1,0:T(8,128)S(1)}, f32[3,256,256]{2,1,0:T(8,128)S(1)}, u32[]{:S(2)}, u32[]{:S(2)}) collective-permute-start(f32[3,256,256]{2,1,0:T(8,128)S(1)} %fusion.30), channel_id=1, source_target_pairs={{0,16},{1,17},{2,18},{3,19},{4,20},{5,21},{6,22},{7,23},{8,24},{9,... | collective-permute-start | bytes 2359304 | tf_op jit(solution)/shard_map/ppermute | solution.py:11
  132.1 88.5 %collective-permute-start.5 = (f32[3,256,256]{2,1,0:T(8,128)S(1)}, f32[3,256,256]{2,1,0:T(8,128)S(1)}, u32[]{:S(2)}, u32[]{:S(2)}) collective-permute-start(f32[3,256,256]{2,1,0:T(8,128)S(1)} %fusion.35), channel_id=1, source_target_pairs={{0,32},{1,33},{2,34},{3,35},{4,36},{5,37},{6,38},{7,39},{8,40},{9,... | collective-permute-start | bytes 2359304 | tf_op jit(solution)/shard_map/ppermute | solution.py:11
  220.7 61.8 %collective-permute-start.6 = (f32[3,256,256]{2,1,0:T(8,128)S(1)}, f32[3,256,256]{2,1,0:T(8,128)S(1)}, u32[]{:S(2)}, u32[]{:S(2)}) collective-permute-start(f32[3,256,256]{2,1,0:T(8,128)S(1)} %add.73), channel_id=1, source_target_pairs={{0,64},{1,65},{2,66},{3,67},{4,68},{5,69},{6,70},{7,71},{8,72},{9,... | collective-permute-start | bytes 2359304 | tf_op jit(solution)/shard_map/ppermute | solution.py:11
  283.3 10.9 %collective-permute-start.7 = (f32[256,224]{0,1:T(8,128)S(1)}, f32[256,224]{0,1:T(8,128)S(1)}, u32[]{:S(2)}, u32[]{:S(2)}) collective-permute-start(f32[256,224]{0,1:T(8,128)S(1)} %slice_select_fusion), channel_id=1, source_target_pairs={{0,4},{1,5},{2,6},{3,7},{4,0},{5,1},{6,2},{7,3},{8,12},{9,13},{10,... | collective-permute-start | bytes 688136 | tf_op jit(solution)/shard_map/ppermute | solution.py:11
  294.3 6.7 %collective-permute-start.8 = (f32[256,112]{0,1:T(8,128)S(1)}, f32[256,112]{0,1:T(8,128)S(1)}, u32[]{:S(2)}, u32[]{:S(2)}) collective-permute-start(f32[256,112]{0,1:T(8,128)S(1)} %slice_select_fusion.1), channel_id=1, source_target_pairs={{0,2},{1,3},{2,0},{3,1},{4,6},{5,7},{6,4},{7,5},{8,10},{9,11},{10,... | collective-permute-start | bytes 344072 | tf_op jit(solution)/shard_map/ppermute | solution.py:11
  301.1 3.1 collective-permute-start.9
  305.1 11.2 %all-to-all-start.2 = ((bf16[8,2,896]{2,1,0:T(2,128)(2,1)}), bf16[8,2,896]{2,1,0:T(2,128)(2,1)S(1)}, u32[]{:S(2)}, u32[]{:S(2)}) async-start(bf16[8,2,896]{2,1,0:T(2,128)(2,1)} %reshape.123), calls=%async_computation.2 | async-start | bytes 57344 | tf_op jit(solution)/shard_map/all_to_all | solution.py:109
where the time goes:
time: 319 us
  waiting for transfers between devices  221 us (69%)
  starting transfers between devices  59.7 us (19%)
  local copies, waits for them, and re-layouts  27 us (8%)
  other arithmetic  5.1 us (2%)
  matrix products  4.32 us (1%)
    ppermute x10, waiting for transfers between devices, from_partner(): lax.ppermute(value, axis, [(i, i ^ 1 << apart) for i in range(lax.axis_si...  203 us
    ppermute x10, starting transfers between devices, from_partner(): lax.ppermute(value, axis, [(i, i ^ 1 << apart) for i in range(lax.axis_si...  45.6 us
    unnamed x30, local copies, waits for them, and re-layouts  22.2 us
    all_to_all x1, waiting for transfers between devices, per_device(): lax.all_to_all(scaled, 'group', split_axis=0, concat_axis=0, tiled=True)  7.74 us
    all_to_all x1, starting transfers between devices, per_device(): lax.all_to_all(x_rows, 'group', split_axis=0, concat_axis=0, tiled=True)  7.23 us
    all_to_all x1, waiting for transfers between devices, per_device(): lax.all_to_all(returned.reshape(group_count, CAP, col_count).astype(jnp.b...  6.91 us
  transfers between devices with their start and end apart: 13, of which 13 were waited for; matrix products, arithmetic and copies ran while one was open for 2% of the time, Pallas kernels for 0%

commit v1 on v0

v1 whole, which is shorter than its diff:
```python
import jax
import jax.numpy as jnp
from jax import lax
from jax.experimental import pallas as pl
from jax.experimental.pallas import tpu as pltpu
from jax.sharding import PartitionSpec as P

EXP_GRP = 32
CAP = 32
NY = 8
NZ = 16
NX = 4
TOK = 512
COLS = 56
FEAT = 448
HID = 256
HALF = 2
ROWS = NY * CAP // HALF
PIECE = CAP // HALF
LANES = 128
MESH = pl.DeviceIdType.MESH
BF16 = jnp.bfloat16
F32 = jnp.float32
FAR_FIRST = (8, 7, 9, 6, 10, 5, 11, 4, 12, 3, 13, 2, 14, 1, 15)
Y_ORDER = (4, 3, 5, 2, 6, 1, 7)
X_ORDER = (1, 3, 2)


def dot(left, right):
    return jnp.dot(left, right, preferred_element_type=F32)


def dot_nt(left, right):
    return lax.dot_general(left, right, (((1,), (1,)), ((), ())), preferred_element_type=F32)


def kernel(
    dy_hbm, x_hbm, ids_hbm, gate_hbm, wg_hbm, wu_hbm, wd_hbm,
    tok_out, og_hbm, ou_hbm, od_hbm,
    dy, xin, ids, gates, wg, wu, wd,
    sel, sel_t, snd, rows, wp_gu, wp_d, part_f, part_b, part_r, hid_r, rows_t,
    dgu, hid, ret, ret_sib, ret_sum, ret_x, home_s, home_r, tok, og, ou, od,
    in_sem, out_sem, y_s, y_r, x_s, x_r, c_s, c_r, rs_s, rs_r, ag_s, ag_r,
    e1_s, e1_r, e2_s, e2_r, f_s, f_r,
):
    y = lax.axis_index("group")
    l = lax.axis_index("local")
    z = l // 8
    j = lax.rem(l, 8)
    x = j // 2
    c = lax.rem(j, 2)

    def at_y(d):
        return (lax.rem(y + d, NY), l)

    def at_z(d):
        return (y, lax.rem(z + d, NZ) * 8 + j)

    def at_x(d):
        return (y, z * 8 + lax.rem(x + d, NX) * 2 + c)

    sib = (y, z * 8 + x * 2 + 1 - c)

    barrier = pltpu.get_barrier_semaphore()
    partners = (
        [at_z(d) for d in FAR_FIRST] + [at_y(d) for d in Y_ORDER] + [at_x(d) for d in X_ORDER] + [sib]
    )
    for who in partners:
        pl.semaphore_signal(barrier, inc=1, device_id=who, device_id_type=MESH)

    loads = [
        pltpu.make_async_copy(src, dst, in_sem.at[num])
        for num, (src, dst) in enumerate(
            (
                (ids_hbm, ids),
                (gate_hbm, gates),
                (x_hbm, xin),
                (dy_hbm, dy),
                (wg_hbm.at[0, 0], wg),
                (wu_hbm.at[0, 0], wu),
                (wd_hbm.at[0, 0], wd),
            )
        )
    ]
    for load in loads:
        load.start()

    def send(src, dst, send_sem, recv_sem, who):
        copy = pltpu.make_async_remote_copy(
            src_ref=src, dst_ref=dst, send_sem=send_sem, recv_sem=recv_sem,
            device_id=who, device_id_type=MESH,
        )
        copy.start()
        return copy

    loads[0].wait()
    loads[1].wait()
    fill = jnp.zeros((TOK, LANES - 8), F32)
    ids_t = jnp.concatenate([ids[...].astype(F32), fill], axis=1).T[:8]
    gates_t = jnp.concatenate([gates[...], fill], axis=1).T[:8]
    target = (lax.broadcasted_iota(jnp.int32, (NY, TOK), 0) * EXP_GRP).astype(F32)
    hit = jnp.zeros((NY, TOK), F32)
    gate_of = jnp.zeros((NY, TOK), F32)
    for k in range(8):
        same = jnp.broadcast_to(ids_t[k : k + 1], (NY, TOK)) == target
        hit = jnp.where(same, 1.0, hit)
        gate_of = gate_of + jnp.where(same, jnp.broadcast_to(gates_t[k : k + 1], (NY, TOK)), 0.0)
    before = (
        lax.broadcasted_iota(jnp.int32, (TOK, TOK), 0) < lax.broadcasted_iota(jnp.int32, (TOK, TOK), 1)
    )
    rank = dot(hit.astype(BF16), jnp.where(before, 1.0, 0.0).astype(BF16))
    rank = jnp.where(hit > 0.0, rank, -1.0)
    loads[2].wait()
    loads[3].wait()
    gap = jnp.zeros((TOK, LANES // 2 - COLS), BF16)
    pair = jnp.concatenate([xin[...], gap, dy[...], gap], axis=1)
    upper = lax.broadcasted_iota(jnp.int32, (ROWS, LANES), 1) >= LANES // 2
    rank_b = jnp.broadcast_to(rank[:, None, :], (NY, PIECE, TOK)).reshape(ROWS, TOK)
    gate_b = jnp.broadcast_to(gate_of[:, None, :], (NY, PIECE, TOK)).reshape(ROWS, TOK)
    slot = lax.rem(lax.broadcasted_iota(jnp.int32, (ROWS, TOK), 0), PIECE).astype(F32)
    for h in range(HALF):
        chosen = rank_b == slot + float(h * PIECE)
        one_hot = jnp.where(chosen, 1.0, 0.0).astype(BF16)
        sel[h * ROWS : (h + 1) * ROWS, :] = one_hot
        slot_gate = jnp.sum(jnp.where(chosen, gate_b, 0.0), axis=1, keepdims=True)
        picked = dot(one_hot, pair)
        picked = jnp.where(upper, slot_gate * picked, picked)
        snd[h] = picked.astype(BF16).reshape(NY, PIECE, LANES)

    pl.semaphore_wait(barrier, len(partners))

    waits = []
    y_copies = [
        send(snd.at[:, lax.rem(y + d, NY)], rows.at[:, j, y], y_s.at[d - 1], y_r.at[d - 1], at_y(d))
        for d in Y_ORDER
    ]
    for h in range(HALF):
        rows[h, j, y] = snd[h, y]

    for load in loads[4:]:
        load.wait()
    zero_rows = jnp.zeros((LANES // 2 - COLS, HID), F32)

    def block(ref, num):
        first = num * COLS
        skip = first % 16
        return jnp.concatenate(
            [ref[first - skip : first + COLS, :].astype(F32)[skip:], zero_rows], axis=0
        ).astype(BF16)

    h0, h1 = slice(0, LANES), slice(LANES, HID)
    for num in range(8):
        low = slice(num * LANES, num * LANES + LANES // 2)
        high = slice(num * LANES + LANES // 2, (num + 1) * LANES)
        g_blk, u_blk, d_blk = block(wg, num), block(wu, num), block(wd, num)
        wp_gu[low, :] = jnp.concatenate([g_blk[:, h0], u_blk[:, h0], g_blk[:, h1], u_blk[:, h1]], axis=1)
        wp_gu[high, :] = jnp.zeros((LANES // 2, 2 * HID), BF16)
        wp_d[low, :] = jnp.zeros((LANES // 2, HID), BF16)
        wp_d[high, :] = d_blk

    for copy in y_copies:
        copy.wait_recv()
    waits += y_copies

    x_copies = []
    c_copies = []
    for h in range(HALF):
        mine = rows.at[h, j]
        x_copies.append({
            d: send(mine, mine, x_s.at[h, d - 1], x_r.at[h, d - 1], at_x(d)) for d in X_ORDER
        })
        c_copies.append({0: send(mine, mine, c_s.at[h, 0], c_r.at[h, 0], sib)})

    rs_copies = []
    for h in range(HALF):
        for d in X_ORDER:
            x_copies[h][d].wait_recv()
            piece = rows.at[h, lax.rem(x + NX - d, NX) * 2 + c]
            c_copies[h][d] = send(piece, piece, c_s.at[h, d], c_r.at[h, d], sib)
        acc_gu = jnp.zeros((ROWS, 2 * HID), F32)
        acc_d = jnp.zeros((ROWS, HID), F32)
        for d in (0,) + X_ORDER:
            c_copies[h][d].wait_recv()
            chip = lax.rem(x + NX - d, NX)
            lhs = jnp.concatenate(
                [rows[h, chip * 2].reshape(ROWS, LANES), rows[h, chip * 2 + 1].reshape(ROWS, LANES)], axis=1
            )
            span = pl.ds(pl.multiple_of(chip * 2 * LANES, 2 * LANES), 2 * LANES)
            acc_gu = acc_gu + dot(lhs, wp_gu[span, :])
            acc_d = acc_d + dot(lhs, wp_d[span, :])
        lo = jnp.concatenate([acc_gu[:, :HID], acc_d[:, :LANES]], axis=1).reshape(NZ, 8, 3 * LANES)
        hi = jnp.concatenate([acc_gu[:, HID:], acc_d[:, LANES:]], axis=1).reshape(NZ, 8, 3 * LANES)
        both = jnp.concatenate([lo, hi], axis=1)
        part_f[h] = both
        part_b[h] = both.astype(BF16)
        rs_copies.append([
            send(part_b.at[h, lax.rem(z + d, NZ)], part_r.at[h, num], rs_s.at[h, num], rs_r.at[h, num], at_z(d))
            for num, d in enumerate(FAR_FIRST)
        ])
        waits += list(x_copies[h].values()) + list(c_copies[h].values())

    sel_t[...] = sel[...].T
    for h in range(HALF):
        for num in range(8):
            rows_t[num * LANES : (num + 1) * LANES, h * ROWS : (h + 1) * ROWS] = (
                rows[h, num].reshape(ROWS, LANES).T
            )

    ag_copies = []
    for h in range(HALF):
        total = part_f[h, z]
        for num in range(NZ - 1):
            rs_copies[h][num].wait_recv()
            total = total + part_r[h, num].astype(F32)
        pre_gate = total[:, :LANES]
        pre_up = total[:, LANES : 2 * LANES]
        back = total[:, 2 * LANES :]
        sigma = 1.0 / (1.0 + jnp.exp(-pre_gate))
        hidden = pre_gate * sigma * pre_up
        d_gate = back * pre_up * sigma * (1.0 + pre_gate * (1.0 - sigma))
        d_up = back * pre_gate * sigma
        hid_r[h, z] = jnp.concatenate([d_gate, d_up, hidden], axis=1).astype(BF16)
        mine = hid_r.at[h, z]
        ag_copies.append([
            send(mine, mine, ag_s.at[h, num], ag_r.at[h, num], at_z(d)) for num, d in enumerate(FAR_FIRST)
        ])
        waits += rs_copies[h]

    low_lane = lax.broadcasted_iota(jnp.int32, (ROWS // 2, LANES), 1) < LANES // 2
    e1_copies = []
    e2_copies = []

    def sum_cores(h):
        e1_copies[h].wait_recv()
        for chip in range(NX):
            ret_sum[h, chip] = ret[h, chip, c] + ret_sib[h, chip]
        e2_copies.append([
            send(ret_sum.at[h, lax.rem(x + d, NX)], ret_x.at[h, d - 1], e2_s.at[h, d - 1], e2_r.at[h, d - 1], at_x(d))
            for d in X_ORDER
        ])

    for h in range(HALF):
        for copy in ag_copies[h]:
            copy.wait_recv()
        waits += ag_copies[h]
        got = hid_r[h].astype(F32)
        lo = got[:, :8].reshape(ROWS, 3 * LANES)
        hi = got[:, 8:].reshape(ROWS, 3 * LANES)
        d_gu = jnp.concatenate([lo[:, :HID], hi[:, :HID]], axis=1).astype(BF16)
        span = slice(h * ROWS, (h + 1) * ROWS)
        dgu[span, :] = d_gu
        hid[span, :] = jnp.concatenate([lo[:, HID:], hi[:, HID:]], axis=1).astype(BF16)
        for num in range(8):
            out = dot_nt(d_gu, wp_gu[num * LANES : (num + 1) * LANES, :])
            ret[h, num // 2, num % 2] = jnp.where(
                low_lane, out[: ROWS // 2], pltpu.roll(out[ROWS // 2 :], LANES // 2, 1)
            )
        e1_copies.append(send(ret.at[h, :, 1 - c], ret_sib.at[h], e1_s.at[h], e1_r.at[h], sib))
        if h == 0:
            sum_cores(0)
    sum_cores(1)
    waits += e1_copies

    gu_all = dgu[...]
    hid_all = hid[...]
    for num in range(8):
        low = slice(num * LANES, num * LANES + LANES // 2)
        high = slice(num * LANES + LANES // 2, (num + 1) * LANES)
        to = slice(num * COLS, (num + 1) * COLS)
        both = dot(rows_t[low, :], gu_all)[:COLS]
        og[to, h0] = both[:, :LANES]
        ou[to, h0] = both[:, LANES:HID]
        og[to, h1] = both[:, HID : HID + LANES]
        ou[to, h1] = both[:, HID + LANES :]
        od[to, :] = dot(rows_t[high, :], hid_all)[:COLS]
    stores = [
        pltpu.make_async_copy(src, dst.at[0, 0], out_sem.at[num])
        for num, (src, dst) in enumerate(((og, og_hbm), (ou, ou_hbm), (od, od_hbm)))
    ]
    for store in stores:
        store.start()

    ends = []
    for h in range(HALF):
        total = ret_sum[h, x]
        for d in X_ORDER:
            e2_copies[h][X_ORDER.index(d)].wait_recv()
            total = total + ret_x[h, d - 1]
        ends.append(total)
        waits += e2_copies[h]
    first = jnp.where(low_lane, ends[0], pltpu.roll(ends[1], LANES // 2, 1))
    second = jnp.where(low_lane, pltpu.roll(ends[0], LANES // 2, 1), ends[1])
    home_s[: NY // 2] = first.astype(BF16).reshape(NY // 2, PIECE, LANES)
    home_s[NY // 2 :] = second.astype(BF16).reshape(NY // 2, PIECE, LANES)
    f_copies = [
        send(home_s.at[lax.rem(y + d, NY)], home_r.at[y], f_s.at[d - 1], f_r.at[d - 1], at_y(d))
        for d in Y_ORDER
    ]
    home_r[y] = home_s[y]
    for copy in waits:
        copy.wait_send()
    for copy in f_copies:
        copy.wait_recv()
    home = home_r[...].reshape(ROWS, LANES)
    both = jnp.concatenate([home.astype(F32), pltpu.roll(home.astype(F32), LANES // 2, 1)], axis=0).astype(BF16)
    tok[...] = dot(sel_t[...], both)[:, :COLS].astype(BF16)
    last = pltpu.make_async_copy(tok, tok_out, out_sem.at[3])
    last.start()
    for copy in f_copies:
        copy.wait_send()
    for store in stores:
        store.wait()
    last.wait()


def per_device(grad_out, tokens_in, expert_ids, gate_values, w_gate, w_up, w_down_t):
    vm = pltpu.VMEM
    dma = pltpu.SemaphoreType.DMA
    scratch = [
        vm((TOK, COLS), BF16), vm((TOK, COLS), BF16), vm((TOK, 8), jnp.int32), vm((TOK, 8), F32),
        vm((FEAT, HID), BF16), vm((FEAT, HID), BF16), vm((FEAT, HID), BF16),
        vm((HALF * ROWS, TOK), BF16),
        vm((TOK, HALF * ROWS), BF16),
        vm((HALF, NY, PIECE, LANES), BF16),
        vm((HALF, 8, NY, PIECE, LANES), BF16),
        vm((8 * LANES, 2 * HID), BF16),
        vm((8 * LANES, HID), BF16),
        vm((HALF, NZ, 16, 3 * LANES), F32),
        vm((HALF, NZ, 16, 3 * LANES), BF16),
        vm((HALF, NZ - 1, 16, 3 * LANES), BF16),
        vm((HALF, NZ, 16, 3 * LANES), BF16),
        vm((8 * LANES, HALF * ROWS), BF16),
        vm((HALF * ROWS, 2 * HID), BF16),
        vm((HALF * ROWS, HID), BF16),
        vm((HALF, NX, 2, ROWS // 2, LANES), F32),
        vm((HALF, NX, ROWS // 2, LANES), F32),
        vm((HALF, NX, ROWS // 2, LANES), F32),
        vm((HALF, NX - 1, ROWS // 2, LANES), F32),
        vm((NY, PIECE, LANES), BF16),
        vm((NY, PIECE, LANES), BF16),
        vm((TOK, COLS), BF16),
        vm((FEAT, HID), F32), vm((FEAT, HID), F32), vm((FEAT, HID), F32),
        dma((7,)), dma((4,)),
        dma((NY - 1,)), dma((NY - 1,)),
        dma((HALF, NX - 1)), dma((HALF, NX - 1)),
        dma((HALF, NX)), dma((HALF, NX)),
        dma((HALF, NZ - 1)), dma((HALF, NZ - 1)),
        dma((HALF, NZ - 1)), dma((HALF, NZ - 1)),
        dma((HALF,)), dma((HALF,)),
        dma((HALF, NX - 1)), dma((HALF, NX - 1)),
        dma((NY - 1,)), dma((NY - 1,)),
    ]
    grad = jax.ShapeDtypeStruct((1, 1, FEAT, HID), F32)
    return pl.pallas_call(
        kernel,
        name="expert_backward",
        out_shape=(jax.ShapeDtypeStruct((TOK, COLS), BF16), grad, grad, grad),
        in_specs=[pl.BlockSpec(memory_space=pl.ANY)] * 7,
        out_specs=[pl.BlockSpec(memory_space=pl.ANY)] * 4,
        scratch_shapes=scratch,
        compiler_params=pltpu.CompilerParams(
            collective_id=0, has_side_effects=True, vmem_limit_bytes=48 << 20
        ),
    )(grad_out, tokens_in, expert_ids, gate_values, w_gate, w_up, w_down_t)


def solution(mesh):
    placed = (
        P("group", "local"),
        P("group", "local"),
        P("group", None),
        P("group", None),
        P("group", "local", None, None),
        P("group", "local", None, None),
        P("group", "local", None, None),
    )
    return jax.shard_map(
        per_device,
        mesh=mesh,
        in_specs=placed,
        out_specs=(
            P("group", "local"),
            P("group", "local", None, None),
            P("group", "local", None, None),
            P("group", "local", None, None),
        ),
        check_vma=False,
    )
```

time: 319 us -> 86.8 us (0.27)
  the two profiles are of different devices: /device:TPU:194 before, /device:TPU:1 now
where the time goes in v1:
time: 86.8 us; the launch traced here: 86.5 us
  Pallas kernels  80.6 us (93%)
  local copies, waits for them, and re-layouts  5.16 us (6%)
    pallas_call x1, Pallas kernels, per_device(): pl.pallas_call(kernel, name='expert_backward', out_shape=(jax.ShapeDtypeS...  80.6 us
    unnamed x19, local copies, waits for them, and re-layouts  4.44 us

profile of v1, /device:TPU:1, one launch (start us, length us, event | category | flops | bytes accessed | tf_op | source)
XLA Modules:
  0.0 86.5 jit_solution(9660231633126300486)
XLA Ops:
  0.6 0.0 copy-start.3
  0.6 0.0 copy-start.4
  0.7 1.0 %copy.11.dy_hbm = bf16[512,56]{1,0:T(8,128)(2,1)S(1)} copy(bf16[512,56]{0,1:T(8,128)(2,1)} %param.7) | data formatting | bytes 114688 | tf_op args[0]
  1.6 0.0 copy-done.3
  1.6 0.0 copy-start.5
  1.6 0.0 copy-start.2
  1.6 0.1 copy.12.x_hbm
  1.8 0.0 copy-done.4
  1.8 0.0 copy-start
  1.8 0.0 copy-start.1
  1.8 0.1 copy.13.ids_hbm
  1.9 0.4 copy-done.5
  2.3 0.1 copy.14.gate_hbm
  2.5 0.1 copy-done.2
  2.6 0.2 copy-done
  2.8 0.1 copy-done.1
  2.9 80.6 %expert_backward.1 = (bf16[512,56]{1,0:T(8,128)(2,1)S(1)}, f32[1,1,448,256]{3,2,1,0:T(8,128)S(1)}, f32[1,1,448,256]{3,2,1,0:T(8,128)S(1)}, f32[1,1,448,256]{3,2,1,0:T(8,128)S(1)}) custom-call(bf16[512,56]{1,0:T(8,128)(2,1)S(1)} %copy.11.dy_hbm, bf16[512,56]{1,0:T(8,128)(2,1)S(1)} %copy.12.x_hbm, s32[512,8]{1,0:T(8,128)S(1)} %copy.13.ids_hbm, ...), custom_call_target="tpu_custom_call" | custom-call | tf_op jit(solution)/shard_map/expert_backward/pallas_call | solution.py:354
  83.5 0.7 copy.15
  84.2 0.8 copy.19
  85.0 0.8 copy.20
  85.8 0.8 copy.21
Async XLA Ops:
  0.6 1.0 %copy-start.3 = (bf16[512,56]{0,1:T(8,128)(2,1)S(1)}, bf16[512,56]{0,1:T(8,128)(2,1)}, u32[]{:S(2)}) copy-start(bf16[512,56]{0,1:T(8,128)(2,1)} %param.8) | copy-start | bytes 172036
  0.6 1.1 %copy-start.4 = (s32[512,8]{0,1:T(8,128)S(1)}, s32[512,8]{0,1:T(8,128)}, u32[]{:S(2)}) copy-start(s32[512,8]{0,1:T(8,128)} %param.9) | copy-start | bytes 49156
  1.6 0.7 copy-start.5
  1.6 0.9 %copy-start.2 = (bf16[1,1,448,256]{3,2,1,0:T(8,128)(2,1)S(1)}, bf16[1,1,448,256]{3,2,1,0:T(8,128)(2,1)}, u32[]{:S(2)}) copy-start(bf16[1,1,448,256]{3,2,1,0:T(8,128)(2,1)} %wd_hbm.1) | copy-start | bytes 688132
  1.8 1.0 %copy-start = (bf16[1,1,448,256]{3,2,1,0:T(8,128)(2,1)S(1)}, bf16[1,1,448,256]{3,2,1,0:T(8,128)(2,1)}, u32[]{:S(2)}) copy-start(bf16[1,1,448,256]{3,2,1,0:T(8,128)(2,1)} %wg_hbm.1) | copy-start | bytes 688132
  1.8 1.1 %copy-start.1 = (bf16[1,1,448,256]{3,2,1,0:T(8,128)(2,1)S(1)}, bf16[1,1,448,256]{3,2,1,0:T(8,128)(2,1)}, u32[]{:S(2)}) copy-start(bf16[1,1,448,256]{3,2,1,0:T(8,128)(2,1)} %wu_hbm.1) | copy-start | bytes 688132

commit v2 on v1

--- a/solution.py
+++ b/solution.py
@@ -19,9 +19,14 @@
 PIECE = CAP // HALF
 LANES = 128
 MESH = pl.DeviceIdType.MESH
+VMEM_FOR_KERNEL = (64 << 20) - 1441792
 BF16 = jnp.bfloat16
 F32 = jnp.float32
-FAR_FIRST = (8, 7, 9, 6, 10, 5, 11, 4, 12, 3, 13, 2, 14, 1, 15)
+QUAD = 4
+FAR = (8, 4, 12)
+AHEAD = (2, 1, 3, 0)
+NEAR = ((2, 1, 15), (14, 1, 15))
+Z_BESIDE = (2, 14, 1, 15)
 Y_ORDER = (4, 3, 5, 2, 6, 1, 7)
 X_ORDER = (1, 3, 2)
 
@@ -38,14 +43,16 @@
     dy_hbm, x_hbm, ids_hbm, gate_hbm, wg_hbm, wu_hbm, wd_hbm,
     tok_out, og_hbm, ou_hbm, od_hbm,
     dy, xin, ids, gates, wg, wu, wd,
-    sel, sel_t, snd, rows, wp_gu, wp_d, part_f, part_b, part_r, hid_r, rows_t,
-    dgu, hid, ret, ret_sib, ret_sum, ret_x, home_s, home_r, tok, og, ou, od,
-    in_sem, out_sem, y_s, y_r, x_s, x_r, c_s, c_r, rs_s, rs_r, ag_s, ag_r,
-    e1_s, e1_r, e2_s, e2_r, f_s, f_r,
+    sel, snd, rows, wp_gu, wp_d, part_f, part_b, near_r, quad_b, far_r, hid_r, rows_t,
+    dgu, hid, ret, ret_sib, ret_sum, ret_send, ret_x, home_s, home_r, tok, og, ou, od,
+    in_sem, out_sem, y_s, y_r, x_s, x_r, c_s, c_r, rn_s, rn_r, rf_s, rf_r, gf_s, gf_r, gn_s, gn_r,
+    e1_s, e1_r, e2_s, e2_r, f_s, f_r, by_two, by_four,
 ):
     y = lax.axis_index("group")
     l = lax.axis_index("local")
     z = l // 8
+    q = lax.rem(z, QUAD)
+    m = z // QUAD
     j = lax.rem(l, 8)
     x = j // 2
     c = lax.rem(j, 2)
@@ -63,7 +70,7 @@
 
     barrier = pltpu.get_barrier_semaphore()
     partners = (
-        [at_z(d) for d in FAR_FIRST] + [at_y(d) for d in Y_ORDER] + [at_x(d) for d in X_ORDER] + [sib]
+        [at_z(d) for d in Z_BESIDE] + [at_y(d) for d in Y_ORDER] + [at_x(d) for d in X_ORDER] + [sib]
     )
     for who in partners:
         pl.semaphore_signal(barrier, inc=1, device_id=who, device_id_type=MESH)
@@ -95,10 +102,9 @@
 
     loads[0].wait()
     loads[1].wait()
-    fill = jnp.zeros((TOK, LANES - 8), F32)
-    ids_t = jnp.concatenate([ids[...].astype(F32), fill], axis=1).T[:8]
-    gates_t = jnp.concatenate([gates[...], fill], axis=1).T[:8]
-    target = (lax.broadcasted_iota(jnp.int32, (NY, TOK), 0) * EXP_GRP).astype(F32)
+    ids_t = ids[...]
+    gates_t = gates[...]
+    target = lax.broadcasted_iota(jnp.int32, (NY, TOK), 0) * EXP_GRP
     hit = jnp.zeros((NY, TOK), F32)
     gate_of = jnp.zeros((NY, TOK), F32)
     for k in range(8):
@@ -112,8 +118,8 @@
     rank = jnp.where(hit > 0.0, rank, -1.0)
     loads[2].wait()
     loads[3].wait()
-    gap = jnp.zeros((TOK, LANES // 2 - COLS), BF16)
-    pair = jnp.concatenate([xin[...], gap, dy[...], gap], axis=1)
+    gap = jnp.zeros((LANES // 2 - COLS, TOK), F32)
+    pair = jnp.concatenate([xin[...].astype(F32), gap, dy[...].astype(F32), gap], axis=0).astype(BF16)
     upper = lax.broadcasted_iota(jnp.int32, (ROWS, LANES), 1) >= LANES // 2
     rank_b = jnp.broadcast_to(rank[:, None, :], (NY, PIECE, TOK)).reshape(ROWS, TOK)
     gate_b = jnp.broadcast_to(gate_of[:, None, :], (NY, PIECE, TOK)).reshape(ROWS, TOK)
@@ -123,11 +129,13 @@
         one_hot = jnp.where(chosen, 1.0, 0.0).astype(BF16)
         sel[h * ROWS : (h + 1) * ROWS, :] = one_hot
         slot_gate = jnp.sum(jnp.where(chosen, gate_b, 0.0), axis=1, keepdims=True)
-        picked = dot(one_hot, pair)
+        picked = dot_nt(one_hot, pair)
         picked = jnp.where(upper, slot_gate * picked, picked)
         snd[h] = picked.astype(BF16).reshape(NY, PIECE, LANES)
 
     pl.semaphore_wait(barrier, len(partners))
+    pl.semaphore_signal(by_two.at[0], inc=1, device_id=at_z(2), device_id_type=MESH)
+    pl.semaphore_signal(by_two.at[1], inc=1, device_id=at_z(14), device_id_type=MESH)
 
     waits = []
     y_copies = [
@@ -171,7 +179,7 @@
         })
         c_copies.append({0: send(mine, mine, c_s.at[h, 0], c_r.at[h, 0], sib)})
 
-    rs_copies = []
+    rn_copies = []
     for h in range(HALF):
         for d in X_ORDER:
             x_copies[h][d].wait_recv()
@@ -190,28 +198,58 @@
             acc_d = acc_d + dot(lhs, wp_d[span, :])
         lo = jnp.concatenate([acc_gu[:, :HID], acc_d[:, :LANES]], axis=1).reshape(NZ, 8, 3 * LANES)
         hi = jnp.concatenate([acc_gu[:, HID:], acc_d[:, LANES:]], axis=1).reshape(NZ, 8, 3 * LANES)
-        both = jnp.concatenate([lo, hi], axis=1)
+        both = jnp.concatenate([lo, hi], axis=1).reshape(QUAD, QUAD, 16, 3 * LANES)
         part_f[h] = both
         part_b[h] = both.astype(BF16)
-        rs_copies.append([
-            send(part_b.at[h, lax.rem(z + d, NZ)], part_r.at[h, num], rs_s.at[h, num], rs_r.at[h, num], at_z(d))
-            for num, d in enumerate(FAR_FIRST)
+        rn_copies.append([
+            [
+                send(
+                    part_b.at[h, lax.rem(z + d, QUAD), lax.rem(lax.rem(z + d, NZ) // QUAD + ahead, QUAD)],
+                    near_r.at[h, num, k], rn_s.at[h, num, k], rn_r.at[h, num, k], at_z(d),
+                )
+                for num, d in enumerate(NEAR[h])
+            ]
+            for k, ahead in enumerate(AHEAD)
         ])
+        if h == 0:
+            pl.semaphore_wait(by_two.at[0], 1)
+            pl.semaphore_wait(by_two.at[1], 1)
+            pl.semaphore_signal(by_four, inc=1, device_id=at_z(4), device_id_type=MESH)
         waits += list(x_copies[h].values()) + list(c_copies[h].values())
 
-    sel_t[...] = sel[...].T
+    rf_copies = []
+    own_sum = []
+    for h in range(HALF):
+        rf_copies.append([])
+        for k, ahead in enumerate(AHEAD):
+            piece = part_f[h, q, lax.rem(m + ahead, QUAD)]
+            for num in range(QUAD - 1):
+                rn_copies[h][k][num].wait_recv()
+                piece = piece + near_r[h, num, k].astype(F32)
+            waits += rn_copies[h][k]
+            if ahead == 0:
+                own_sum.append(piece)
+                continue
+            quad_b[h, k] = piece.astype(BF16)
+            if h == 0 and k == 0:
+                pl.semaphore_wait(by_four, 1)
+            rf_copies[h].append(
+                send(quad_b.at[h, k], far_r.at[h, k], rf_s.at[h, k], rf_r.at[h, k], at_z(FAR[k]))
+            )
+
     for h in range(HALF):
         for num in range(8):
             rows_t[num * LANES : (num + 1) * LANES, h * ROWS : (h + 1) * ROWS] = (
                 rows[h, num].reshape(ROWS, LANES).T
             )
 
-    ag_copies = []
-    for h in range(HALF):
-        total = part_f[h, z]
-        for num in range(NZ - 1):
-            rs_copies[h][num].wait_recv()
-            total = total + part_r[h, num].astype(F32)
+    gf_copies = []
+    gn_copies = []
+    for h in range(HALF):
+        total = own_sum[h]
+        for num in range(QUAD - 1):
+            rf_copies[h][num].wait_recv()
+            total = total + far_r[h, num].astype(F32)
         pre_gate = total[:, :LANES]
         pre_up = total[:, LANES : 2 * LANES]
         back = total[:, 2 * LANES :]
@@ -219,12 +257,23 @@
         hidden = pre_gate * sigma * pre_up
         d_gate = back * pre_up * sigma * (1.0 + pre_gate * (1.0 - sigma))
         d_up = back * pre_gate * sigma
-        hid_r[h, z] = jnp.concatenate([d_gate, d_up, hidden], axis=1).astype(BF16)
-        mine = hid_r.at[h, z]
-        ag_copies.append([
-            send(mine, mine, ag_s.at[h, num], ag_r.at[h, num], at_z(d)) for num, d in enumerate(FAR_FIRST)
+        hid_r[h, q, m] = jnp.concatenate([d_gate, d_up, hidden], axis=1).astype(BF16)
+        mine = hid_r.at[h, q, m]
+        gf_copies.append([
+            send(mine, mine, gf_s.at[h, num], gf_r.at[h, num], at_z(d)) for num, d in enumerate(FAR)
         ])
-        waits += rs_copies[h]
+        gn_copies.append([
+            send(mine, mine, gn_s.at[h, 3, num], gn_r.at[h, 3, num], at_z(d)) for num, d in enumerate(NEAR[h])
+        ])
+        waits += rf_copies[h]
+
+    for k, h in ((1, 0), (2, 0), (1, 1), (2, 1), (0, 0), (0, 1)):
+        gf_copies[h][k].wait_recv()
+        waits.append(gf_copies[h][k])
+        piece = hid_r.at[h, q, lax.rem(m + QUAD - AHEAD[k], QUAD)]
+        gn_copies[h] += [
+            send(piece, piece, gn_s.at[h, k, num], gn_r.at[h, k, num], at_z(d)) for num, d in enumerate(NEAR[h])
+        ]
 
     low_lane = lax.broadcasted_iota(jnp.int32, (ROWS // 2, LANES), 1) < LANES // 2
     e1_copies = []
@@ -233,17 +282,19 @@
     def sum_cores(h):
         e1_copies[h].wait_recv()
         for chip in range(NX):
-            ret_sum[h, chip] = ret[h, chip, c] + ret_sib[h, chip]
+            total = ret[h, chip, c] + ret_sib[h, chip]
+            ret_sum[h, chip] = total
+            ret_send[h, chip] = total.astype(BF16)
         e2_copies.append([
-            send(ret_sum.at[h, lax.rem(x + d, NX)], ret_x.at[h, d - 1], e2_s.at[h, d - 1], e2_r.at[h, d - 1], at_x(d))
+            send(ret_send.at[h, lax.rem(x + d, NX)], ret_x.at[h, d - 1], e2_s.at[h, d - 1], e2_r.at[h, d - 1], at_x(d))
             for d in X_ORDER
         ])
 
     for h in range(HALF):
-        for copy in ag_copies[h]:
+        for copy in gn_copies[h]:
             copy.wait_recv()
-        waits += ag_copies[h]
-        got = hid_r[h].astype(F32)
+        waits += gn_copies[h]
+        got = hid_r[h].reshape(NZ, 16, 3 * LANES).astype(F32)
         lo = got[:, :8].reshape(ROWS, 3 * LANES)
         hi = got[:, 8:].reshape(ROWS, 3 * LANES)
         d_gu = jnp.concatenate([lo[:, :HID], hi[:, :HID]], axis=1).astype(BF16)
@@ -285,7 +336,7 @@
         total = ret_sum[h, x]
         for d in X_ORDER:
             e2_copies[h][X_ORDER.index(d)].wait_recv()
-            total = total + ret_x[h, d - 1]
+            total = total + ret_x[h, d - 1].astype(F32)
         ends.append(total)
         waits += e2_copies[h]
     first = jnp.where(low_lane, ends[0], pltpu.roll(ends[1], LANES // 2, 1))
@@ -301,9 +352,9 @@
         copy.wait_send()
     for copy in f_copies:
         copy.wait_recv()
-    home = home_r[...].reshape(ROWS, LANES)
-    both = jnp.concatenate([home.astype(F32), pltpu.roll(home.astype(F32), LANES // 2, 1)], axis=0).astype(BF16)
-    tok[...] = dot(sel_t[...], both)[:, :COLS].astype(BF16)
+    home = home_r[...].reshape(ROWS, LANES).astype(F32).T
+    both = jnp.concatenate([home[: LANES // 2], home[LANES // 2 :]], axis=1).astype(BF16)
+    tok[...] = dot(both, sel[...])[:COLS].astype(BF16)
     last = pltpu.make_async_copy(tok, tok_out, out_sem.at[3])
     last.start()
     for copy in f_copies:
@@ -313,55 +364,79 @@
     last.wait()
 
 
+def hand_over(*refs):
+    count = len(refs) // 2
+    sems = refs[-1]
+    copies = [pltpu.make_async_copy(refs[i], refs[count + i], sems.at[i]) for i in range(count)]
+    for copy in copies:
+        copy.start()
+    for copy in copies:
+        copy.wait()
+
+
 def per_device(grad_out, tokens_in, expert_ids, gate_values, w_gate, w_up, w_down_t):
     vm = pltpu.VMEM
     dma = pltpu.SemaphoreType.DMA
     scratch = [
-        vm((TOK, COLS), BF16), vm((TOK, COLS), BF16), vm((TOK, 8), jnp.int32), vm((TOK, 8), F32),
+        vm((COLS, TOK), BF16), vm((COLS, TOK), BF16), vm((8, TOK), jnp.int32), vm((8, TOK), F32),
         vm((FEAT, HID), BF16), vm((FEAT, HID), BF16), vm((FEAT, HID), BF16),
         vm((HALF * ROWS, TOK), BF16),
-        vm((TOK, HALF * ROWS), BF16),
         vm((HALF, NY, PIECE, LANES), BF16),
         vm((HALF, 8, NY, PIECE, LANES), BF16),
         vm((8 * LANES, 2 * HID), BF16),
         vm((8 * LANES, HID), BF16),
-        vm((HALF, NZ, 16, 3 * LANES), F32),
-        vm((HALF, NZ, 16, 3 * LANES), BF16),
-        vm((HALF, NZ - 1, 16, 3 * LANES), BF16),
-        vm((HALF, NZ, 16, 3 * LANES), BF16),
+        vm((HALF, QUAD, QUAD, 16, 3 * LANES), F32),
+        vm((HALF, QUAD, QUAD, 16, 3 * LANES), BF16),
+        vm((HALF, QUAD - 1, QUAD, 16, 3 * LANES), BF16),
+        vm((HALF, QUAD - 1, 16, 3 * LANES), BF16),
+        vm((HALF, QUAD - 1, 16, 3 * LANES), BF16),
+        vm((HALF, QUAD, QUAD, 16, 3 * LANES), BF16),
         vm((8 * LANES, HALF * ROWS), BF16),
         vm((HALF * ROWS, 2 * HID), BF16),
         vm((HALF * ROWS, HID), BF16),
         vm((HALF, NX, 2, ROWS // 2, LANES), F32),
         vm((HALF, NX, ROWS // 2, LANES), F32),
         vm((HALF, NX, ROWS // 2, LANES), F32),
-        vm((HALF, NX - 1, ROWS // 2, LANES), F32),
+        vm((HALF, NX, ROWS // 2, LANES), BF16),
+        vm((HALF, NX - 1, ROWS // 2, LANES), BF16),
         vm((NY, PIECE, LANES), BF16),
         vm((NY, PIECE, LANES), BF16),
-        vm((TOK, COLS), BF16),
+        vm((COLS, TOK), BF16),
         vm((FEAT, HID), F32), vm((FEAT, HID), F32), vm((FEAT, HID), F32),
         dma((7,)), dma((4,)),
         dma((NY - 1,)), dma((NY - 1,)),
         dma((HALF, NX - 1)), dma((HALF, NX - 1)),
         dma((HALF, NX)), dma((HALF, NX)),
-        dma((HALF, NZ - 1)), dma((HALF, NZ - 1)),
-        dma((HALF, NZ - 1)), dma((HALF, NZ - 1)),
+        dma((HALF, QUAD - 1, QUAD)), dma((HALF, QUAD - 1, QUAD)),
+        dma((HALF, QUAD - 1)), dma((HALF, QUAD - 1)),
+        dma((HALF, QUAD - 1)), dma((HALF, QUAD - 1)),
+        dma((HALF, QUAD, QUAD - 1)), dma((HALF, QUAD, QUAD - 1)),
         dma((HALF,)), dma((HALF,)),
         dma((HALF, NX - 1)), dma((HALF, NX - 1)),
         dma((NY - 1,)), dma((NY - 1,)),
+        pltpu.SemaphoreType.REGULAR((2,)), pltpu.SemaphoreType.REGULAR,
     ]
     grad = jax.ShapeDtypeStruct((1, 1, FEAT, HID), F32)
-    return pl.pallas_call(
+    found = pl.pallas_call(
         kernel,
         name="expert_backward",
-        out_shape=(jax.ShapeDtypeStruct((TOK, COLS), BF16), grad, grad, grad),
-        in_specs=[pl.BlockSpec(memory_space=pl.ANY)] * 7,
-        out_specs=[pl.BlockSpec(memory_space=pl.ANY)] * 4,
+        out_shape=(jax.ShapeDtypeStruct((COLS, TOK), BF16), grad, grad, grad),
+        in_specs=[pl.BlockSpec(memory_space=pltpu.HBM)] * 7,
+        out_specs=[pl.BlockSpec(memory_space=pltpu.HBM)] * 4,
         scratch_shapes=scratch,
         compiler_params=pltpu.CompilerParams(
-            collective_id=0, has_side_effects=True, vmem_limit_bytes=48 << 20
+            collective_id=0, has_side_effects=True, vmem_limit_bytes=VMEM_FOR_KERNEL
         ),
-    )(grad_out, tokens_in, expert_ids, gate_values, w_gate, w_up, w_down_t)
+    )(grad_out.T, tokens_in.T, expert_ids.T, gate_values.T, w_gate, w_up, w_down_t)
+    tok_t, d_gate, d_up, d_down = pl.pallas_call(
+        hand_over,
+        name="hand_over",
+        out_shape=[jax.ShapeDtypeStruct(each.shape, each.dtype) for each in found],
+        in_specs=[pl.BlockSpec(memory_space=pltpu.VMEM)] * 4,
+        out_specs=[pl.BlockSpec(memory_space=pl.ANY)] * 4,
+        scratch_shapes=[dma((4,))],
+    )(*found)
+    return tok_t.T, d_gate, d_up, d_down
 
 
 def solution(mesh):

time: 86.8 us -> 71.8 us (0.83)
  Pallas kernels: 80.6 us -> 70.9 us
  local copies, waits for them, and re-layouts: 5.16 us -> 0 us
    pallas_call x1, Pallas kernels: 80.6 us -> 68.4 us  [per_device(): pl.pallas_call(kernel, name='expert_backward', out_shape=(jax.ShapeDtypeS...]
    unnamed x19 -> x0, local copies, waits for them, and re-layouts: 4.44 us -> none
    pallas_call x0 -> x1, Pallas kernels: none -> 2.45 us  [per_device(): pl.pallas_call(hand_over, name='hand_over', out_shape=[jax.ShapeDtypeStru...]
where the time goes in v2:
time: 71.8 us; the launch traced here: 71.5 us
  Pallas kernels  70.9 us (99%)
    pallas_call x1, Pallas kernels, per_device(): pl.pallas_call(kernel, name='expert_backward', out_shape=(jax.ShapeDtypeS...  68.4 us
    pallas_call x1, Pallas kernels, per_device(): pl.pallas_call(hand_over, name='hand_over', out_shape=[jax.ShapeDtypeStru...  2.45 us

profile of v2, /device:TPU:1, one launch (start us, length us, event | category | flops | bytes accessed | tf_op | source)
XLA Modules:
  0.0 71.5 jit_solution(7766948389653133474)
XLA Ops:
  0.6 68.4 %expert_backward.1 = (bf16[56,512]{1,0:T(8,128)(2,1)}, f32[1,1,448,256]{3,2,1,0:T(8,128)}, f32[1,1,448,256]{3,2,1,0:T(8,128)}, f32[1,1,448,256]{3,2,1,0:T(8,128)}) custom-call(bf16[56,512]{1,0:T(8,128)(2,1)} %bitcast.5, bf16[56,512]{1,0:T(8,128)(2,1)} %bitcast.6, s32[8,512]{1,0:T(8,128)} %bitcast.7, f32[8,512]{1,0:T(8,128)} %bitcast.8, ...), custom_call_target="tpu_custom_call" | custom-call | tf_op jit(solution)/shard_map/expert_backward/pallas_call | solution.py:420
  69.1 2.4 %hand_over.1 = (bf16[56,512]{1,0:T(8,128)(2,1)}, f32[1,1,448,256]{3,2,1,0:T(8,128)}, f32[1,1,448,256]{3,2,1,0:T(8,128)}, f32[1,1,448,256]{3,2,1,0:T(8,128)}) custom-call(bf16[56,512]{1,0:T(8,128)(2,1)} %get-tuple-element.12.refs_0_, f32[1,1,448,256]{3,2,1,0:T(8,128)} %get-tuple-element.13.refs_1_, f32[1,1,448,256]{3,2,1,0:T(8,128)} %get-tuple-element.14.refs_2_, ...), custom_call_target="tpu_custom_call" | custom-call | tf_op jit(solution)/shard_map/hand_over/pallas_call | solution.py:431

commit v3 on v2

--- a/solution.py
+++ b/solution.py
@@ -23,11 +23,13 @@
 BF16 = jnp.bfloat16
 F32 = jnp.float32
 QUAD = 4
-FAR = (8, 4, 12)
-AHEAD = (2, 1, 3, 0)
+FAR = ((0, 8), (1, 12), (3, 4))
+OWN = 2
+CUTS = (slice(0, 1), slice(1, 4))
 NEAR = ((2, 1, 15), (14, 1, 15))
 Z_BESIDE = (2, 14, 1, 15)
 Y_ORDER = (4, 3, 5, 2, 6, 1, 7)
+Y_SPLIT = ((0, 1, 7, 2), (6, 3, 5, 4))
 X_ORDER = (1, 3, 2)
 
 
@@ -43,7 +45,7 @@
     dy_hbm, x_hbm, ids_hbm, gate_hbm, wg_hbm, wu_hbm, wd_hbm,
     tok_out, og_hbm, ou_hbm, od_hbm,
     dy, xin, ids, gates, wg, wu, wd,
-    sel, snd, rows, wp_gu, wp_d, part_f, part_b, near_r, quad_b, far_r, hid_r, rows_t,
+    sel, snd, rows, wp_gu, wp_d, part_f, part_b, near_r, quad_b, far_r, mine_r, near_g, spread, rows_t,
     dgu, hid, ret, ret_sib, ret_sum, ret_send, ret_x, home_s, home_r, tok, og, ou, od,
     in_sem, out_sem, y_s, y_r, x_s, x_r, c_s, c_r, rn_s, rn_r, rf_s, rf_r, gf_s, gf_r, gn_s, gn_r,
     e1_s, e1_r, e2_s, e2_r, f_s, f_r, by_two, by_four,
@@ -131,19 +133,20 @@
         slot_gate = jnp.sum(jnp.where(chosen, gate_b, 0.0), axis=1, keepdims=True)
         picked = dot_nt(one_hot, pair)
         picked = jnp.where(upper, slot_gate * picked, picked)
-        snd[h] = picked.astype(BF16).reshape(NY, PIECE, LANES)
+        snd[:, h * PIECE : (h + 1) * PIECE] = picked.astype(BF16).reshape(NY, PIECE, LANES)
 
     pl.semaphore_wait(barrier, len(partners))
     pl.semaphore_signal(by_two.at[0], inc=1, device_id=at_z(2), device_id_type=MESH)
     pl.semaphore_signal(by_two.at[1], inc=1, device_id=at_z(14), device_id_type=MESH)
 
     waits = []
-    y_copies = [
-        send(snd.at[:, lax.rem(y + d, NY)], rows.at[:, j, y], y_s.at[d - 1], y_r.at[d - 1], at_y(d))
-        for d in Y_ORDER
-    ]
-    for h in range(HALF):
-        rows[h, j, y] = snd[h, y]
+    y_copies = {}
+    for d in Y_ORDER:
+        h = 0 if d in Y_SPLIT[0] else 1
+        y_copies[d] = send(
+            snd.at[lax.rem(y + d, NY)], rows.at[h, j, Y_SPLIT[h].index(d)], y_s.at[d - 1], y_r.at[d - 1], at_y(d)
+        )
+    rows[0, j, 0] = snd[y]
 
     for load in loads[4:]:
         load.wait()
@@ -166,25 +169,26 @@
         wp_d[low, :] = jnp.zeros((LANES // 2, HID), BF16)
         wp_d[high, :] = d_blk
 
-    for copy in y_copies:
-        copy.wait_recv()
-    waits += y_copies
-
     x_copies = []
     c_copies = []
     for h in range(HALF):
+        for d in Y_SPLIT[h]:
+            if d > 0:
+                y_copies[d].wait_recv()
         mine = rows.at[h, j]
         x_copies.append({
             d: send(mine, mine, x_s.at[h, d - 1], x_r.at[h, d - 1], at_x(d)) for d in X_ORDER
         })
         c_copies.append({0: send(mine, mine, c_s.at[h, 0], c_r.at[h, 0], sib)})
-
-    rn_copies = []
+    waits += list(y_copies.values())
     for h in range(HALF):
         for d in X_ORDER:
             x_copies[h][d].wait_recv()
             piece = rows.at[h, lax.rem(x + NX - d, NX) * 2 + c]
             c_copies[h][d] = send(piece, piece, c_s.at[h, d], c_r.at[h, d], sib)
+
+    rn_copies = []
+    for h in range(HALF):
         acc_gu = jnp.zeros((ROWS, 2 * HID), F32)
         acc_d = jnp.zeros((ROWS, HID), F32)
         for d in (0,) + X_ORDER:
@@ -199,17 +203,23 @@
         lo = jnp.concatenate([acc_gu[:, :HID], acc_d[:, :LANES]], axis=1).reshape(NZ, 8, 3 * LANES)
         hi = jnp.concatenate([acc_gu[:, HID:], acc_d[:, LANES:]], axis=1).reshape(NZ, 8, 3 * LANES)
         both = jnp.concatenate([lo, hi], axis=1).reshape(QUAD, QUAD, 16, 3 * LANES)
-        part_f[h] = both
-        part_b[h] = both.astype(BF16)
+        for num in range(QUAD):
+            apart = lax.rem(num + QUAD - q, QUAD)
+            step = jnp.where(apart == 3, NZ - 1, jnp.where(apart == 2, NEAR[h][0], apart))
+            lead = lax.rem(z + step, NZ) // QUAD
+            for part in range(QUAD):
+                place = lax.rem(part + 2 * QUAD - lead + 2, QUAD)
+                part_f[h, num, place] = both[num, part]
+                part_b[h, num, place] = both[num, part].astype(BF16)
         rn_copies.append([
             [
                 send(
-                    part_b.at[h, lax.rem(z + d, QUAD), lax.rem(lax.rem(z + d, NZ) // QUAD + ahead, QUAD)],
-                    near_r.at[h, num, k], rn_s.at[h, num, k], rn_r.at[h, num, k], at_z(d),
+                    part_b.at[h, lax.rem(z + d, QUAD), cut], near_r.at[h, num, cut],
+                    rn_s.at[h, num, k], rn_r.at[h, num, k], at_z(d),
                 )
                 for num, d in enumerate(NEAR[h])
             ]
-            for k, ahead in enumerate(AHEAD)
+            for k, cut in enumerate(CUTS)
         ])
         if h == 0:
             pl.semaphore_wait(by_two.at[0], 1)
@@ -219,23 +229,25 @@
 
     rf_copies = []
     own_sum = []
-    for h in range(HALF):
-        rf_copies.append([])
-        for k, ahead in enumerate(AHEAD):
-            piece = part_f[h, q, lax.rem(m + ahead, QUAD)]
+    for k, cut in enumerate(CUTS):
+        for h in range(HALF):
+            total = part_f[h, q, cut]
             for num in range(QUAD - 1):
                 rn_copies[h][k][num].wait_recv()
-                piece = piece + near_r[h, num, k].astype(F32)
+                total = total + near_r[h, num, cut].astype(F32)
             waits += rn_copies[h][k]
-            if ahead == 0:
-                own_sum.append(piece)
-                continue
-            quad_b[h, k] = piece.astype(BF16)
+            if k == 0:
+                rf_copies.append({})
+            else:
+                own_sum.append(total[OWN - cut.start])
+            quad_b[h, cut] = total.astype(BF16)
             if h == 0 and k == 0:
                 pl.semaphore_wait(by_four, 1)
-            rf_copies[h].append(
-                send(quad_b.at[h, k], far_r.at[h, k], rf_s.at[h, k], rf_r.at[h, k], at_z(FAR[k]))
-            )
+            for place, d in FAR:
+                if cut.start <= place < cut.stop:
+                    rf_copies[h][place] = send(
+                        quad_b.at[h, place], far_r.at[h, place], rf_s.at[h, place], rf_r.at[h, place], at_z(d)
+                    )
 
     for h in range(HALF):
         for num in range(8):
@@ -247,9 +259,9 @@
     gn_copies = []
     for h in range(HALF):
         total = own_sum[h]
-        for num in range(QUAD - 1):
-            rf_copies[h][num].wait_recv()
-            total = total + far_r[h, num].astype(F32)
+        for place, d in reversed(FAR):
+            rf_copies[h][place].wait_recv()
+            total = total + far_r[h, place].astype(F32)
         pre_gate = total[:, :LANES]
         pre_up = total[:, LANES : 2 * LANES]
         back = total[:, 2 * LANES :]
@@ -257,23 +269,27 @@
         hidden = pre_gate * sigma * pre_up
         d_gate = back * pre_up * sigma * (1.0 + pre_gate * (1.0 - sigma))
         d_up = back * pre_gate * sigma
-        hid_r[h, q, m] = jnp.concatenate([d_gate, d_up, hidden], axis=1).astype(BF16)
-        mine = hid_r.at[h, q, m]
-        gf_copies.append([
-            send(mine, mine, gf_s.at[h, num], gf_r.at[h, num], at_z(d)) for num, d in enumerate(FAR)
-        ])
-        gn_copies.append([
-            send(mine, mine, gn_s.at[h, 3, num], gn_r.at[h, 3, num], at_z(d)) for num, d in enumerate(NEAR[h])
-        ])
-        waits += rf_copies[h]
-
-    for k, h in ((1, 0), (2, 0), (1, 1), (2, 1), (0, 0), (0, 1)):
-        gf_copies[h][k].wait_recv()
-        waits.append(gf_copies[h][k])
-        piece = hid_r.at[h, q, lax.rem(m + QUAD - AHEAD[k], QUAD)]
-        gn_copies[h] += [
-            send(piece, piece, gn_s.at[h, k, num], gn_r.at[h, k, num], at_z(d)) for num, d in enumerate(NEAR[h])
-        ]
+        mine_r[h, OWN] = jnp.concatenate([d_gate, d_up, hidden], axis=1).astype(BF16)
+        gf_copies.append({
+            place: send(mine_r.at[h, OWN], mine_r.at[h, place], gf_s.at[h, place], gf_r.at[h, place], at_z(NZ - d))
+            for place, d in FAR
+        })
+        waits += list(rf_copies[h].values())
+
+    for k in (1, 0):
+        for h in range(HALF):
+            for place, d in FAR:
+                if CUTS[k].start <= place < CUTS[k].stop:
+                    gf_copies[h][place].wait_recv()
+            if k == 1:
+                waits += list(gf_copies[h].values())
+                gn_copies.append([])
+            gn_copies[h] += [
+                send(
+                    mine_r.at[h, CUTS[k]], near_g.at[h, num, CUTS[k]], gn_s.at[h, num, k], gn_r.at[h, num, k], at_z(d)
+                )
+                for num, d in enumerate(NEAR[h])
+            ]
 
     low_lane = lax.broadcasted_iota(jnp.int32, (ROWS // 2, LANES), 1) < LANES // 2
     e1_copies = []
@@ -294,9 +310,15 @@
         for copy in gn_copies[h]:
             copy.wait_recv()
         waits += gn_copies[h]
-        got = hid_r[h].reshape(NZ, 16, 3 * LANES).astype(F32)
-        lo = got[:, :8].reshape(ROWS, 3 * LANES)
-        hi = got[:, 8:].reshape(ROWS, 3 * LANES)
+        for num in range(QUAD):
+            owner = z if num == QUAD - 1 else lax.rem(z + NZ - NEAR[h][num], NZ)
+            for place in range(QUAD):
+                got = (mine_r[h, place] if num == QUAD - 1 else near_g[h, num, place]).astype(F32)
+                rank_of = lax.rem(owner, QUAD) * QUAD + lax.rem(owner // QUAD + place + 2, QUAD)
+                spread[h, rank_of] = jnp.concatenate([got[:8], got[8:]], axis=1)
+        whole = spread[h].reshape(ROWS, 6 * LANES)
+        lo = whole[:, : 3 * LANES]
+        hi = whole[:, 3 * LANES :]
         d_gu = jnp.concatenate([lo[:, :HID], hi[:, :HID]], axis=1).astype(BF16)
         span = slice(h * ROWS, (h + 1) * ROWS)
         dgu[span, :] = d_gu
@@ -307,11 +329,40 @@
                 low_lane, out[: ROWS // 2], pltpu.roll(out[ROWS // 2 :], LANES // 2, 1)
             )
         e1_copies.append(send(ret.at[h, :, 1 - c], ret_sib.at[h], e1_s.at[h], e1_r.at[h], sib))
-        if h == 0:
-            sum_cores(0)
+    sum_cores(0)
     sum_cores(1)
     waits += e1_copies
 
+    f_copies = []
+    low_piece = lax.broadcasted_iota(jnp.int32, (PIECE, LANES), 1) < LANES // 2
+
+    def return_rows(h):
+        total = ret_sum[h, x]
+        for num, d in enumerate(X_ORDER):
+            e2_copies[h][num].wait_recv()
+            total = total + ret_x[h, d - 1].astype(F32)
+        turned = pltpu.roll(total, LANES // 2, 1)
+        for num, d in enumerate(Y_SPLIT[h]):
+            first = CAP * (num % 2)
+            one = slice(first, first + PIECE)
+            two = slice(first + PIECE, first + CAP)
+            if num < 2:
+                block_out = jnp.where(low_piece, total[one], turned[two])
+            else:
+                block_out = jnp.where(low_piece, turned[one], total[two])
+            home_s[h, num] = block_out.astype(BF16)
+            if d == 0:
+                home_r[y] = home_s[h, num]
+            else:
+                f_copies.append(
+                    send(home_s.at[h, num], home_r.at[y], f_s.at[d - 1], f_r.at[d - 1], at_y(NY - d))
+                )
+
+    return_rows(0)
+
+    return_rows(1)
+    for h in range(HALF):
+        waits += e2_copies[h]
     gu_all = dgu[...]
     hid_all = hid[...]
     for num in range(8):
@@ -331,23 +382,6 @@
     for store in stores:
         store.start()
 
-    ends = []
-    for h in range(HALF):
-        total = ret_sum[h, x]
-        for d in X_ORDER:
-            e2_copies[h][X_ORDER.index(d)].wait_recv()
-            total = total + ret_x[h, d - 1].astype(F32)
-        ends.append(total)
-        waits += e2_copies[h]
-    first = jnp.where(low_lane, ends[0], pltpu.roll(ends[1], LANES // 2, 1))
-    second = jnp.where(low_lane, pltpu.roll(ends[0], LANES // 2, 1), ends[1])
-    home_s[: NY // 2] = first.astype(BF16).reshape(NY // 2, PIECE, LANES)
-    home_s[NY // 2 :] = second.astype(BF16).reshape(NY // 2, PIECE, LANES)
-    f_copies = [
-        send(home_s.at[lax.rem(y + d, NY)], home_r.at[y], f_s.at[d - 1], f_r.at[d - 1], at_y(d))
-        for d in Y_ORDER
-    ]
-    home_r[y] = home_s[y]
     for copy in waits:
         copy.wait_send()
     for copy in f_copies:
@@ -365,13 +399,16 @@
 
 
 def hand_over(*refs):
-    count = len(refs) // 2
-    sems = refs[-1]
-    copies = [pltpu.make_async_copy(refs[i], refs[count + i], sems.at[i]) for i in range(count)]
-    for copy in copies:
-        copy.start()
-    for copy in copies:
-        copy.wait()
+    found, given, held, sems = refs[:4], refs[4:8], refs[8:12], refs[12]
+    loads = [pltpu.make_async_copy(found[i], held[i], sems.at[0, i]) for i in range(4)]
+    stores = [pltpu.make_async_copy(held[i], given[i], sems.at[1, i]) for i in range(4)]
+    for load in loads:
+        load.start()
+    for load, store in zip(loads, stores):
+        load.wait()
+        store.start()
+    for store in stores:
+        store.wait()
 
 
 def per_device(grad_out, tokens_in, expert_ids, gate_values, w_gate, w_up, w_down_t):
@@ -381,16 +418,18 @@
         vm((COLS, TOK), BF16), vm((COLS, TOK), BF16), vm((8, TOK), jnp.int32), vm((8, TOK), F32),
         vm((FEAT, HID), BF16), vm((FEAT, HID), BF16), vm((FEAT, HID), BF16),
         vm((HALF * ROWS, TOK), BF16),
-        vm((HALF, NY, PIECE, LANES), BF16),
-        vm((HALF, 8, NY, PIECE, LANES), BF16),
+        vm((NY, CAP, LANES), BF16),
+        vm((HALF, 8, NY // 2, CAP, LANES), BF16),
         vm((8 * LANES, 2 * HID), BF16),
         vm((8 * LANES, HID), BF16),
         vm((HALF, QUAD, QUAD, 16, 3 * LANES), F32),
         vm((HALF, QUAD, QUAD, 16, 3 * LANES), BF16),
         vm((HALF, QUAD - 1, QUAD, 16, 3 * LANES), BF16),
-        vm((HALF, QUAD - 1, 16, 3 * LANES), BF16),
-        vm((HALF, QUAD - 1, 16, 3 * LANES), BF16),
-        vm((HALF, QUAD, QUAD, 16, 3 * LANES), BF16),
+        vm((HALF, QUAD, 16, 3 * LANES), BF16),
+        vm((HALF, QUAD, 16, 3 * LANES), BF16),
+        vm((HALF, QUAD, 16, 3 * LANES), BF16),
+        vm((HALF, QUAD - 1, QUAD, 16, 3 * LANES), BF16),
+        vm((HALF, NZ, 8, 6 * LANES), F32),
         vm((8 * LANES, HALF * ROWS), BF16),
         vm((HALF * ROWS, 2 * HID), BF16),
         vm((HALF * ROWS, HID), BF16),
@@ -399,7 +438,7 @@
         vm((HALF, NX, ROWS // 2, LANES), F32),
         vm((HALF, NX, ROWS // 2, LANES), BF16),
         vm((HALF, NX - 1, ROWS // 2, LANES), BF16),
-        vm((NY, PIECE, LANES), BF16),
+        vm((HALF, NY // 2, PIECE, LANES), BF16),
         vm((NY, PIECE, LANES), BF16),
         vm((COLS, TOK), BF16),
         vm((FEAT, HID), F32), vm((FEAT, HID), F32), vm((FEAT, HID), F32),
@@ -407,10 +446,10 @@
         dma((NY - 1,)), dma((NY - 1,)),
         dma((HALF, NX - 1)), dma((HALF, NX - 1)),
         dma((HALF, NX)), dma((HALF, NX)),
-        dma((HALF, QUAD - 1, QUAD)), dma((HALF, QUAD - 1, QUAD)),
-        dma((HALF, QUAD - 1)), dma((HALF, QUAD - 1)),
-        dma((HALF, QUAD - 1)), dma((HALF, QUAD - 1)),
-        dma((HALF, QUAD, QUAD - 1)), dma((HALF, QUAD, QUAD - 1)),
+        dma((HALF, QUAD - 1, 2)), dma((HALF, QUAD - 1, 2)),
+        dma((HALF, QUAD)), dma((HALF, QUAD)),
+        dma((HALF, QUAD)), dma((HALF, QUAD)),
+        dma((HALF, QUAD - 1, 2)), dma((HALF, QUAD - 1, 2)),
         dma((HALF,)), dma((HALF,)),
         dma((HALF, NX - 1)), dma((HALF, NX - 1)),
         dma((NY - 1,)), dma((NY - 1,)),
@@ -432,9 +471,9 @@
         hand_over,
         name="hand_over",
         out_shape=[jax.ShapeDtypeStruct(each.shape, each.dtype) for each in found],
-        in_specs=[pl.BlockSpec(memory_space=pltpu.VMEM)] * 4,
+        in_specs=[pl.BlockSpec(memory_space=pl.ANY)] * 4,
         out_specs=[pl.BlockSpec(memory_space=pl.ANY)] * 4,
-        scratch_shapes=[dma((4,))],
+        scratch_shapes=[vm(each.shape, each.dtype) for each in found] + [dma((2, 4))],
     )(*found)
     return tok_t.T, d_gate, d_up, d_down
 

time: 71.8 us -> 69.4 us (0.967)
  Pallas kernels: 70.9 us -> 68.5 us
    pallas_call x1, Pallas kernels: 68.4 us -> 66.3 us  [per_device(): pl.pallas_call(kernel, name='expert_backward', out_shape=(jax.ShapeDtypeS...]
where the time goes in v3:
time: 69.4 us; the launch traced here: 69.2 us
  Pallas kernels  68.5 us (99%)
    pallas_call x1, Pallas kernels, per_device(): pl.pallas_call(kernel, name='expert_backward', out_shape=(jax.ShapeDtypeS...  66.3 us
    pallas_call x1, Pallas kernels, per_device(): pl.pallas_call(hand_over, name='hand_over', out_shape=[jax.ShapeDtypeStru...  2.19 us

profile of v3, /device:TPU:1, one launch (start us, length us, event | category | flops | bytes accessed | tf_op | source)
XLA Modules:
  0.0 69.2 jit_solution(10725743408294048988)
XLA Ops:
  0.6 66.3 %expert_backward.1 = (bf16[56,512]{1,0:T(8,128)(2,1)}, f32[1,1,448,256]{3,2,1,0:T(8,128)}, f32[1,1,448,256]{3,2,1,0:T(8,128)}, f32[1,1,448,256]{3,2,1,0:T(8,128)}) custom-call(bf16[56,512]{1,0:T(8,128)(2,1)} %bitcast.5, bf16[56,512]{1,0:T(8,128)(2,1)} %bitcast.6, s32[8,512]{1,0:T(8,128)} %bitcast.7, f32[8,512]{1,0:T(8,128)} %bitcast.8, ...), custom_call_target="tpu_custom_call" | custom-call | tf_op jit(solution)/shard_map/expert_backward/pallas_call | solution.py:459
  67.0 2.2 %hand_over.1 = (bf16[56,512]{1,0:T(8,128)(2,1)}, f32[1,1,448,256]{3,2,1,0:T(8,128)}, f32[1,1,448,256]{3,2,1,0:T(8,128)}, f32[1,1,448,256]{3,2,1,0:T(8,128)}) custom-call(bf16[56,512]{1,0:T(8,128)(2,1)} %get-tuple-element.12.refs_0_, f32[1,1,448,256]{3,2,1,0:T(8,128)} %get-tuple-element.13.refs_1_, f32[1,1,448,256]{3,2,1,0:T(8,128)} %get-tuple-element.14.refs_2_, ...), custom_call_target="tpu_custom_call" | custom-call | tf_op jit(solution)/shard_map/hand_over/pallas_call | solution.py:470

commit v4 on v3

--- a/solution.py
+++ b/solution.py
@@ -43,10 +43,10 @@
 
 def kernel(
     dy_hbm, x_hbm, ids_hbm, gate_hbm, wg_hbm, wu_hbm, wd_hbm,
-    tok_out, og_hbm, ou_hbm, od_hbm,
+    home_r, sel_hbm, og_hbm, ou_hbm, od_hbm,
     dy, xin, ids, gates, wg, wu, wd,
     sel, snd, rows, wp_gu, wp_d, part_f, part_b, near_r, quad_b, far_r, mine_r, near_g, spread, rows_t,
-    dgu, hid, ret, ret_sib, ret_sum, ret_send, ret_x, home_s, home_r, tok, og, ou, od,
+    dgu, hid, ret, ret_sib, ret_sum, ret_send, ret_x, home_s, og, ou, od,
     in_sem, out_sem, y_s, y_r, x_s, x_r, c_s, c_r, rn_s, rn_r, rf_s, rf_r, gf_s, gf_r, gn_s, gn_r,
     e1_s, e1_r, e2_s, e2_r, f_s, f_r, by_two, by_four,
 ):
@@ -135,6 +135,8 @@
         picked = jnp.where(upper, slot_gate * picked, picked)
         snd[:, h * PIECE : (h + 1) * PIECE] = picked.astype(BF16).reshape(NY, PIECE, LANES)
 
+    keep_sel = pltpu.make_async_copy(sel, sel_hbm, out_sem.at[3])
+    keep_sel.start()
     pl.semaphore_wait(barrier, len(partners))
     pl.semaphore_signal(by_two.at[0], inc=1, device_id=at_z(2), device_id_type=MESH)
     pl.semaphore_signal(by_two.at[1], inc=1, device_id=at_z(14), device_id_type=MESH)
@@ -334,6 +336,7 @@
     waits += e1_copies
 
     f_copies = []
+    own_rows = []
     low_piece = lax.broadcasted_iota(jnp.int32, (PIECE, LANES), 1) < LANES // 2
 
     def return_rows(h):
@@ -352,7 +355,8 @@
                 block_out = jnp.where(low_piece, turned[one], total[two])
             home_s[h, num] = block_out.astype(BF16)
             if d == 0:
-                home_r[y] = home_s[h, num]
+                own_rows.append(pltpu.make_async_copy(home_s.at[h, num], home_r.at[y], out_sem.at[4]))
+                own_rows[0].start()
             else:
                 f_copies.append(
                     send(home_s.at[h, num], home_r.at[y], f_s.at[d - 1], f_r.at[d - 1], at_y(NY - d))
@@ -386,25 +390,36 @@
         copy.wait_send()
     for copy in f_copies:
         copy.wait_recv()
-    home = home_r[...].reshape(ROWS, LANES).astype(F32).T
-    both = jnp.concatenate([home[: LANES // 2], home[LANES // 2 :]], axis=1).astype(BF16)
-    tok[...] = dot(both, sel[...])[:COLS].astype(BF16)
-    last = pltpu.make_async_copy(tok, tok_out, out_sem.at[3])
-    last.start()
     for copy in f_copies:
         copy.wait_send()
     for store in stores:
         store.wait()
-    last.wait()
-
-
-def hand_over(*refs):
-    found, given, held, sems = refs[:4], refs[4:8], refs[8:12], refs[12]
-    loads = [pltpu.make_async_copy(found[i], held[i], sems.at[0, i]) for i in range(4)]
-    stores = [pltpu.make_async_copy(held[i], given[i], sems.at[1, i]) for i in range(4)]
+    keep_sel.wait()
+    own_rows[0].wait()
+
+
+def scatter_rows(
+    home_hbm, sel_hbm, og_hbm, ou_hbm, od_hbm, tok_out, og_out, ou_out, od_out, home_r, sel, og, ou, od, tok, sems
+):
+    loads = [
+        pltpu.make_async_copy(src, dst, sems.at[0, num])
+        for num, (src, dst) in enumerate(
+            ((home_hbm, home_r), (sel_hbm, sel), (og_hbm, og), (ou_hbm, ou), (od_hbm, od))
+        )
+    ]
+    stores = [
+        pltpu.make_async_copy(src, dst, sems.at[1, num])
+        for num, (src, dst) in enumerate(((tok, tok_out), (og, og_out), (ou, ou_out), (od, od_out)))
+    ]
     for load in loads:
         load.start()
-    for load, store in zip(loads, stores):
+    loads[0].wait()
+    loads[1].wait()
+    home = home_r[...].reshape(ROWS, LANES).astype(F32).T
+    both = jnp.concatenate([home[: LANES // 2], home[LANES // 2 :]], axis=1).astype(BF16)
+    tok[...] = dot(both, sel[...])[:COLS].astype(BF16)
+    stores[0].start()
+    for load, store in zip(loads[2:], stores[1:]):
         load.wait()
         store.start()
     for store in stores:
@@ -439,10 +454,8 @@
         vm((HALF, NX, ROWS // 2, LANES), BF16),
         vm((HALF, NX - 1, ROWS // 2, LANES), BF16),
         vm((HALF, NY // 2, PIECE, LANES), BF16),
-        vm((NY, PIECE, LANES), BF16),
-        vm((COLS, TOK), BF16),
         vm((FEAT, HID), F32), vm((FEAT, HID), F32), vm((FEAT, HID), F32),
-        dma((7,)), dma((4,)),
+        dma((7,)), dma((5,)),
         dma((NY - 1,)), dma((NY - 1,)),
         dma((HALF, NX - 1)), dma((HALF, NX - 1)),
         dma((HALF, NX)), dma((HALF, NX)),
@@ -459,21 +472,27 @@
     found = pl.pallas_call(
         kernel,
         name="expert_backward",
-        out_shape=(jax.ShapeDtypeStruct((COLS, TOK), BF16), grad, grad, grad),
+        out_shape=(
+            jax.ShapeDtypeStruct((NY, PIECE, LANES), BF16),
+            jax.ShapeDtypeStruct((HALF * ROWS, TOK), BF16),
+            grad,
+            grad,
+            grad,
+        ),
         in_specs=[pl.BlockSpec(memory_space=pltpu.HBM)] * 7,
-        out_specs=[pl.BlockSpec(memory_space=pltpu.HBM)] * 4,
+        out_specs=[pl.BlockSpec(memory_space=pltpu.HBM)] * 5,
         scratch_shapes=scratch,
         compiler_params=pltpu.CompilerParams(
             collective_id=0, has_side_effects=True, vmem_limit_bytes=VMEM_FOR_KERNEL
         ),
     )(grad_out.T, tokens_in.T, expert_ids.T, gate_values.T, w_gate, w_up, w_down_t)
     tok_t, d_gate, d_up, d_down = pl.pallas_call(
-        hand_over,
-        name="hand_over",
-        out_shape=[jax.ShapeDtypeStruct(each.shape, each.dtype) for each in found],
-        in_specs=[pl.BlockSpec(memory_space=pl.ANY)] * 4,
+        scatter_rows,
+        name="scatter_rows",
+        out_shape=[jax.ShapeDtypeStruct((COLS, TOK), BF16), grad, grad, grad],
+        in_specs=[pl.BlockSpec(memory_space=pl.ANY)] * 5,
         out_specs=[pl.BlockSpec(memory_space=pl.ANY)] * 4,
-        scratch_shapes=[vm(each.shape, each.dtype) for each in found] + [dma((2, 4))],
+        scratch_shapes=[vm(each.shape, each.dtype) for each in found] + [vm((COLS, TOK), BF16), dma((2, 5))],
     )(*found)
     return tok_t.T, d_gate, d_up, d_down
 

time: 69.4 us -> 69.1 us (level)
  no operation moved by 1% of the time
where the time goes in v4:
time: 69.1 us; the launch traced here: 68.9 us
  Pallas kernels  68.2 us (99%)
    pallas_call x1, Pallas kernels, per_device(): pl.pallas_call(kernel, name='expert_backward', out_shape=(jax.ShapeDtypeS...  65.8 us
    pallas_call x1, Pallas kernels, per_device(): pl.pallas_call(scatter_rows, name='scatter_rows', out_shape=[jax.ShapeDty...  2.37 us

profile of v4, /device:TPU:1, one launch (start us, length us, event | category | flops | bytes accessed | tf_op | source)
XLA Modules:
  0.0 68.9 jit_solution(11063241528901003514)
XLA Ops:
  0.6 65.8 %expert_backward.1 = (bf16[8,16,128]{2,1,0:T(8,128)(2,1)}, bf16[256,512]{1,0:T(8,128)(2,1)}, f32[1,1,448,256]{3,2,1,0:T(8,128)}, f32[1,1,448,256]{3,2,1,0:T(8,128)}, f32[1,1,448,256]{3,2,1,0:T(8,128)}) custom-call(bf16[56,512]{1,0:T(8,128)(2,1)} %bitcast.5, bf16[56,512]{1,0:T(8,128)(2,1)} %bitcast.6, s32[8,512]{1,0:T(8,128)} %bitcast.7, f32[8,512]{1,0:T(8,128)} %bitcast.8, ...), custom_call_target="tpu_custom_call" | custom-call | tf_op jit(solution)/shard_map/expert_backward/pallas_call | solution.py:472
  66.5 2.4 %scatter_rows.1 = (bf16[56,512]{1,0:T(8,128)(2,1)}, f32[1,1,448,256]{3,2,1,0:T(8,128)}, f32[1,1,448,256]{3,2,1,0:T(8,128)}, f32[1,1,448,256]{3,2,1,0:T(8,128)}) custom-call(bf16[8,16,128]{2,1,0:T(8,128)(2,1)} %get-tuple-element.13.home_hbm, bf16[256,512]{1,0:T(8,128)(2,1)} %get-tuple-element.14.sel_hbm, f32[1,1,448,256]{3,2,1,0:T(8,128)} %get-tuple-element.15.og_hbm, ...), custom_call_target="tpu_custom_call" | custom-call | tf_op jit(solution)/shard_map/scatter_rows/pallas_call | solution.py:489
